TPU v7x, 256 devices: a whole 4x4x8 slice. The times are simulated.
256 devices in a mesh: dp: 8 (over x, core), expert: 32 (over z, y).
Axes of the slice: x: 4, y: 4, z: 8, core: 2. Of those that a mesh axis runs over, the one named last changes fastest.
Arguments:
- tokens: bfloat16 [256, 3584], P('expert', 'dp'), may hold values from -6 to 6
- d_out: bfloat16 [256, 3584], P('expert', 'dp'), may hold values from -6 to 6
- gate_dense: bfloat16 [3584, 12288], P('expert', 'dp'), may hold values from -0.09375 to 0.09375
- up_dense: bfloat16 [3584, 12288], P('expert', 'dp'), may hold values from -0.09375 to 0.09375
- down_dense: bfloat16 [12288, 3584], P('dp', 'expert'), may hold values from -0.125 to 0.125
- block_map: int32 [32, 16], replicated, may hold values from 0 to 95, as said below
- routes: int32 [256, 8], P('expert'), may hold values from 0 to 31, all different within a row; in each aligned block of 8 rows (0 to 7, 8 to 15, ...) at most 4 rows name the same one
- route_gates: float32 [8], replicated, may hold values from 0.1 to 1
Outputs:
- mixed: bfloat16 [256, 3584], P('expert', 'dp')
- d_tokens: bfloat16 [256, 3584], P('expert', 'dp')
- gate_dense_grad: float32 [3584, 12288], P('expert', 'dp')
- up_dense_grad: float32 [3584, 12288], P('expert', 'dp')
- down_dense_grad: float32 [12288, 3584], P('dp', 'expert')
Inputs may be any that keep to these rules, and one draw needn't show every extreme that they name: `block_map`: for every expert and every j below 8, the entries j * 2 to (j + 1) * 2 - 1 of its row are different blocks of the old shard j, numbered j * 12 to (j + 1) * 12 - 1. Among the 8 tokens of one index of expert, no expert is named by more than 4 routes, and in every draw some expert is named by exactly 4 routes of some such block.
All inputs are finite; a program needn't handle non-finite values.
Results may differ from a plain program's by a relative error of at most 0.019.
Values may be sent and summed in bfloat16 or wider, within the bound.
A program may use at most 128 MiB of HBM per device.

v0:
```python
import jax
import jax.numpy as jnp
from jax import lax
from jax.sharding import PartitionSpec as P

BLK = 128


def contract(left, right, left_dim, right_dim):
    return lax.dot_general(
        left, right, (((left_dim,), (right_dim,)), ((), ())), preferred_element_type=jnp.float32
    )


def shards(tokens, d_out, gate_dense, up_dense, down_dense, block_map, routes, route_gates):
    dp_count = lax.axis_size("dp")
    ex_count = lax.axis_size("expert")
    dp_index = lax.axis_index("dp")
    experts_all = block_map.shape[0]
    exp_local = experts_all // ex_count
    per_group = block_map.shape[1] // dp_count
    dense_width = gate_dense.shape[1]
    blocks_owned = dense_width // BLK
    rows_owned = gate_dense.shape[0]
    model_width = rows_owned * ex_count
    tok_count, route_count = routes.shape
    capacity = 2 * tok_count * route_count // experts_all
    block_total = exp_local * per_group
    owned_map = lax.dynamic_slice_in_dim(block_map, dp_index * per_group, per_group, 1)
    local_picks = owned_map - dp_index * blocks_owned
    gate_send = jnp.transpose(
        jnp.take(gate_dense.reshape(rows_owned, blocks_owned, BLK), local_picks, axis=1),
        (1, 0, 2, 3),
    )
    up_send = jnp.transpose(
        jnp.take(up_dense.reshape(rows_owned, blocks_owned, BLK), local_picks, axis=1), (1, 0, 2, 3)
    )
    down_send = jnp.take(down_dense.reshape(blocks_owned, BLK, rows_owned), local_picks, axis=0)
    gate_recv, up_recv, down_recv = (
        lax.all_to_all(gate_send, "expert", split_axis=0, concat_axis=0, tiled=True),
        lax.all_to_all(up_send, "expert", split_axis=0, concat_axis=0, tiled=True),
        lax.all_to_all(down_send, "expert", split_axis=0, concat_axis=0, tiled=True),
    )
    w_gate = gate_recv.reshape(model_width, block_total * BLK)
    w_up = up_recv.reshape(model_width, block_total * BLK)
    w_down = jnp.transpose(down_recv, (1, 2, 0, 3)).reshape(block_total * BLK, model_width)
    span = tok_count * route_count
    flat_routes = routes.reshape(span)
    labels = jnp.arange(experts_all, dtype=jnp.int32)
    onehot = (flat_routes[:, None] == labels[None, :]).astype(jnp.int32)
    slot_rank = jnp.sum(jnp.cumsum(onehot, axis=0) * onehot, axis=1) - 1
    target_slot = flat_routes * capacity + slot_rank
    slot_route = (
        jnp.full((experts_all * capacity,), span, jnp.int32)
        .at[target_slot]
        .set(jnp.arange(span, dtype=jnp.int32))
    )
    slot_token = slot_route // route_count
    slot_choice = slot_route % route_count
    choice_match = slot_choice[:, None] == jnp.arange(route_count, dtype=jnp.int32)[None, :]
    slot_gate = jnp.sum(jnp.where(choice_match, route_gates[None, :], 0.0), axis=1)
    slot_gate = jnp.where(slot_route < span, slot_gate, 0.0)
    full_tokens, full_cotan = (
        lax.all_gather(tokens, "dp", axis=1, tiled=True),
        lax.all_gather(d_out, "dp", axis=1, tiled=True),
    )
    feature_count = full_tokens.shape[1]
    blank = jnp.zeros((1, feature_count), jnp.bfloat16)
    picked_tokens = jnp.take(jnp.concatenate([full_tokens, blank], axis=0), slot_token, axis=0)
    picked_cotan = jnp.take(jnp.concatenate([full_cotan, blank], axis=0), slot_token, axis=0)
    scaled = (slot_gate[:, None] * picked_cotan.astype(jnp.float32)).astype(jnp.bfloat16)
    layout = (ex_count, exp_local, capacity, feature_count)
    token_slots = picked_tokens.reshape(layout)
    cotan_slots = scaled.reshape(layout)
    x_in, dy_in = (
        lax.all_to_all(token_slots, "expert", split_axis=0, concat_axis=0, tiled=True),
        lax.all_to_all(cotan_slots, "expert", split_axis=0, concat_axis=0, tiled=True),
    )
    x_rows = x_in[:, 0].reshape(ex_count * capacity, model_width)
    dy_rows = dy_in[:, 0].reshape(ex_count * capacity, model_width)
    gate_pre = jnp.dot(x_rows, w_gate, preferred_element_type=jnp.float32)
    up_pre = jnp.dot(x_rows, w_up, preferred_element_type=jnp.float32)
    silu_gate = jax.nn.silu(gate_pre)
    hidden = (silu_gate * up_pre).astype(jnp.bfloat16)
    out_part = jnp.dot(hidden, w_down, preferred_element_type=jnp.float32)
    hidden_grad = contract(dy_rows, w_down, 1, 1)
    sigma = jax.nn.sigmoid(gate_pre)
    gate_grad = (hidden_grad * up_pre * sigma * (1.0 + gate_pre * (1.0 - sigma))).astype(
        jnp.bfloat16
    )
    up_grad = (hidden_grad * silu_gate).astype(jnp.bfloat16)
    in_part = contract(gate_grad, w_gate, 1, 1) + contract(up_grad, w_up, 1, 1)
    gate_grads = contract(x_rows, gate_grad, 0, 0).astype(jnp.bfloat16)
    up_grads = contract(x_rows, up_grad, 0, 0).astype(jnp.bfloat16)
    down_grads = contract(hidden, dy_rows, 0, 0).astype(jnp.bfloat16)
    out_parts = [out_part.reshape(ex_count, capacity, model_width)]
    in_parts = [in_part.reshape(ex_count, capacity, model_width)]
    out_stack = jnp.stack(out_parts, axis=1)
    in_stack = jnp.stack(in_parts, axis=1)
    out_summed, in_summed = (
        lax.psum_scatter(
            out_stack.astype(jnp.bfloat16), "dp", scatter_dimension=3, tiled=True
        ).astype(jnp.float32),
        lax.psum_scatter(
            in_stack.astype(jnp.bfloat16), "dp", scatter_dimension=3, tiled=True
        ).astype(jnp.float32),
    )
    out_back, in_back = (
        lax.all_to_all(
            out_summed.astype(jnp.bfloat16), "expert", split_axis=0, concat_axis=0, tiled=True
        ),
        lax.all_to_all(
            in_summed.astype(jnp.bfloat16), "expert", split_axis=0, concat_axis=0, tiled=True
        ),
    )
    share_width = out_back.shape[3]
    out_flat = out_back.reshape(experts_all * capacity, share_width)
    in_flat = in_back.reshape(experts_all * capacity, share_width)
    out_routes = jnp.take(out_flat, target_slot, axis=0).reshape(
        tok_count, route_count, share_width
    )
    in_routes = jnp.take(in_flat, target_slot, axis=0).reshape(tok_count, route_count, share_width)
    mixed = jnp.sum(route_gates[None, :, None] * out_routes.astype(jnp.float32), axis=1).astype(
        jnp.bfloat16
    )
    d_tokens = jnp.sum(in_routes.astype(jnp.float32), axis=1).astype(jnp.bfloat16)
    gate_back = gate_grads.reshape(ex_count, rows_owned, block_total, BLK)
    up_back = up_grads.reshape(ex_count, rows_owned, block_total, BLK)
    down_back = jnp.transpose(
        down_grads.reshape(block_total, BLK, ex_count, rows_owned), (2, 0, 1, 3)
    )
    gate_home, up_home, down_home = (
        lax.all_to_all(gate_back, "expert", split_axis=0, concat_axis=0, tiled=True),
        lax.all_to_all(up_back, "expert", split_axis=0, concat_axis=0, tiled=True),
        lax.all_to_all(down_back, "expert", split_axis=0, concat_axis=0, tiled=True),
    )
    selector = (
        local_picks[:, :, None] == jnp.arange(blocks_owned, dtype=jnp.int32)[None, None, :]
    ).astype(jnp.bfloat16)
    gate_dense_grad = jnp.einsum(
        "esm,ersb->rmb", selector, gate_home, preferred_element_type=jnp.float32
    ).reshape(rows_owned, dense_width)
    up_dense_grad = jnp.einsum(
        "esm,ersb->rmb", selector, up_home, preferred_element_type=jnp.float32
    ).reshape(rows_owned, dense_width)
    down_dense_grad = jnp.einsum(
        "esm,esbr->mbr", selector, down_home, preferred_element_type=jnp.float32
    ).reshape(dense_width, rows_owned)
    return (mixed, d_tokens, gate_dense_grad, up_dense_grad, down_dense_grad)


def solution(mesh):
    in_specs = (
        P("expert", "dp"),
        P("expert", "dp"),
        P("expert", "dp"),
        P("expert", "dp"),
        P("dp", "expert"),
        P(),
        P("expert", None),
        P(),
    )
    out_specs = (
        P("expert", "dp"),
        P("expert", "dp"),
        P("expert", "dp"),
        P("expert", "dp"),
        P("dp", "expert"),
    )
    return jax.shard_map(shards, mesh=mesh, in_specs=in_specs, out_specs=out_specs, check_vma=False)
```

profile of v0, /device:TPU:2, one launch (start us, length us, event | category | flops | bytes accessed | tf_op | source)
XLA Modules:
  0.0 556.8 jit_solution(3008810786125094768)
XLA Ops:
  8.6 13.0 %all-gather = bf16[8,448,8]{1,2,0:T(8,128)(2,1)S(1)} all-gather(bf16[1,448,8]{1,2,0:T(8,128)(2,1)} %bitcast.133), channel_id=1, replica_groups=mesh['dp'=8,'expert'=32] {'dp'}, dimensions={0}, use_global_device_ids=true | all-gather | bytes 64512 | tf_op jit(solution)/shard_map/all_gather | solution.py:64
  25.5 11.5 %all-to-all-start = ((bf16[32,1,4,3584]{3,2,1,0:T(4,128)(2,1)}), bf16[32,1,4,3584]{3,2,1,0:T(4,128)(2,1)S(1)}, u32[]{:S(2)}, u32[]{:S(2)}) async-start(bf16[32,1,4,3584]{3,2,1,0:T(4,128)(2,1)} %bitcast.5), calls=%async_computation | async-start | bytes 1835008 | tf_op jit(solution)/shard_map/all_to_all | solution.py:76
  37.1 12.8 %all-gather.1 = bf16[8,448,8]{1,2,0:T(8,128)(2,1)S(1)} all-gather(bf16[1,448,8]{1,2,0:T(8,128)(2,1)S(1)} %bitcast.134), channel_id=1, replica_groups=mesh['dp'=8,'expert'=32] {'dp'}, dimensions={0}, use_global_device_ids=true | all-gather | bytes 64512 | tf_op jit(solution)/shard_map/all_gather | solution.py:65
  52.7 10.1 %all-to-all-done = bf16[32,1,4,3584]{3,2,1,0:T(4,128)(2,1)S(1)} async-done(((bf16[32,1,4,3584]{3,2,1,0:T(4,128)(2,1)}), bf16[32,1,4,3584]{3,2,1,0:T(4,128)(2,1)S(1)}, u32[]{:S(2)}, u32[]{:S(2)}) %all-to-all-start) | async-done | bytes 917536 | tf_op jit(solution)/shard_map/all_to_all | solution.py:76
  62.8 5.5 all-to-all-start.5
  72.2 20.5 %all-to-all-done.5 = bf16[32,1,4,3584]{3,2,1,0:T(4,128)(2,1)S(1)} async-done(((bf16[32,1,4,3584]{3,2,1,0:T(4,128)(2,1)}), bf16[32,1,4,3584]{3,2,1,0:T(4,128)(2,1)S(1)}, u32[]{:S(2)}, u32[]{:S(2)}) %all-to-all-start.5) | async-done | bytes 917536 | tf_op jit(solution)/shard_map/all_to_all | solution.py:77
  93.6 5.5 all-to-all-start.3
  104.2 7.5 %fusion.2 = (bf16[32,112,2,128]{3,2,1,0:T(2,128)(2,1)}, bf16[32,112,2,128]{3,2,1,0:T(2,128)(2,1)}) fusion(pred[32,2]{1,0:T(8,128)(4,1)S(1)} %copy.89, bf16[32,2,112,128]{3,2,1,0:T(8,128)(2,1)} %bitcast.122, bf16[32,2,112,128]{3,2,1,0:T(8,128)(2,1)} %bitcast.123), kind=kLoop, calls=%fused_computation.17 | loop fusion | flops 1835008 | bytes 7340096 | tf_op jit(solution)/shard_map/transpose | solution.py:31
  111.7 30.8 %all-to-all-done.3 = bf16[32,2,128,112]{2,3,1,0:T(8,128)(2,1)S(1)} async-done(((bf16[32,2,128,112]{2,3,1,0:T(8,128)(2,1)}), bf16[32,2,128,112]{2,3,1,0:T(8,128)(2,1)S(1)}, u32[]{:S(2)}, u32[]{:S(2)}) %all-to-all-start.3) | async-done | bytes 1835040 | tf_op jit(solution)/shard_map/all_to_all | solution.py:42
  143.7 49.1 %all_to_all.50 = bf16[32,112,2,128]{3,2,1,0:T(2,128)(2,1)S(1)} all-to-all(bf16[32,112,2,128]{3,2,1,0:T(2,128)(2,1)} %get-tuple-element.32), channel_id=1, replica_groups=mesh['dp'=8,'expert'=32] {'expert'}, dimensions={0} | all-to-all | bytes 3670016 | tf_op jit(solution)/shard_map/all_to_all | solution.py:40
  192.9 5.1 all-to-all-start.2
  202.3 4.2 copy.103
  206.9 33.3 %all-to-all-done.2 = bf16[32,112,2,128]{3,2,1,0:T(2,128)(2,1)} async-done(((bf16[32,112,2,128]{3,2,1,0:T(2,128)(2,1)}), bf16[32,112,2,128]{3,2,1,0:T(2,128)(2,1)}, u32[]{:S(2)}, u32[]{:S(2)}) %all-to-all-start.2) | async-done | bytes 1835040 | tf_op jit(solution)/shard_map/all_to_all | solution.py:41
  242.9 3.2 fusion.1
  246.1 5.5 copy.126
  251.6 5.5 reshape.258
  260.4 24.6 %copy.128 = bf16[32,1,4,3584]{2,0,1,3:T(8,128)(2,1)} copy(bf16[32,1,4,3584]{3,2,0,1:T(4,128)(2,1)S(1)} %convert_element_type.75) | data formatting | bytes 1835008
  285.0 54.3 %reshape.260 = bf16[3584,128]{1,0:T(8,128)(2,1)} reshape(bf16[3584,1,32,4]{3,2,1,0:T(8,128)(2,1)} %bitcast.112) | data formatting | bytes 1835008
  341.4 6.1 %all-to-all-start.4 = ((bf16[32,1,4,448]{3,2,1,0:T(4,128)(2,1)}), bf16[32,1,4,448]{3,2,1,0:T(4,128)(2,1)S(1)}, u32[]{:S(2)}, u32[]{:S(2)}) async-start(bf16[32,1,4,448]{3,2,1,0:T(4,128)(2,1)} %copy.106), calls=%async_computation.4 | async-start | bytes 262144 | tf_op jit(solution)/shard_map/all_to_all | solution.py:109
  347.5 20.1 %reduce-scatter.9.cloned.1.call-done = bf16[448,128]{1,0:T(8,128)(2,1)} async-done(((bf16[3584,128]{1,0:T(8,128)(2,1)}), bf16[448,128]{1,0:T(8,128)(2,1)}) %reduce-scatter.9.cloned.1.call-update) | async-done | bytes 114704
  367.6 9.6 %reshape.261 = bf16[448,1,32,4]{3,2,1,0:T(8,128)(2,1)} reshape(bf16[448,128]{1,0:T(8,128)(2,1)} %reduce-scatter.9.cloned.1.call-done) | data formatting | bytes 229376
  377.2 5.3 copy.129
  382.5 9.7 %all-to-all-start.6 = ((bf16[32,1,4,448]{3,2,1,0:T(4,128)(2,1)}), bf16[32,1,4,448]{3,2,1,0:T(4,128)(2,1)S(1)}, u32[]{:S(2)}, u32[]{:S(2)}) async-start(bf16[32,1,4,448]{3,2,1,0:T(4,128)(2,1)} %bitcast.24), calls=%async_computation.6 | async-start | bytes 262144 | tf_op jit(solution)/shard_map/all_to_all | solution.py:112
  394.3 8.4 %all-to-all-done.6 = bf16[32,1,4,448]{3,2,1,0:T(4,128)(2,1)S(1)} async-done(((bf16[32,1,4,448]{3,2,1,0:T(4,128)(2,1)}), bf16[32,1,4,448]{3,2,1,0:T(4,128)(2,1)S(1)}, u32[]{:S(2)}, u32[]{:S(2)}) %all-to-all-start.6) | async-done | bytes 114720 | tf_op jit(solution)/shard_map/all_to_all | solution.py:112
  402.7 4.0 all-to-all-start.7
  408.7 4.6 reshape.153
  413.2 36.9 %all-to-all-done.7 = bf16[32,112,2,128]{3,2,1,0:T(2,128)(2,1)S(1)} async-done(((bf16[32,112,2,128]{3,2,1,0:T(2,128)(2,1)}), bf16[32,112,2,128]{3,2,1,0:T(2,128)(2,1)S(1)}, u32[]{:S(2)}, u32[]{:S(2)}) %all-to-all-start.7) | async-done | bytes 1835040 | tf_op jit(solution)/shard_map/all_to_all | solution.py:133
  451.4 5.4 all-to-all-start.8
  458.7 4.2 reshape.257
  465.8 33.0 %all-to-all-done.8 = bf16[32,112,2,128]{3,2,1,0:T(2,128)(2,1)} async-done(((bf16[32,112,2,128]{3,2,1,0:T(2,128)(2,1)}), bf16[32,112,2,128]{3,2,1,0:T(2,128)(2,1)}, u32[]{:S(2)}, u32[]{:S(2)}) %all-to-all-start.8) | async-done | bytes 1835040 | tf_op jit(solution)/shard_map/all_to_all | solution.py:134
  498.8 6.2 %all-to-all-start.9 = ((bf16[32,2,128,112]{2,1,3,0:T(2,128)(2,1)}), bf16[32,2,128,112]{2,1,3,0:T(2,128)(2,1)}, u32[]{:S(2)}, u32[]{:S(2)}) async-start(bf16[32,2,128,112]{2,1,3,0:T(2,128)(2,1)} %bitcast.119), calls=%async_computation.9 | async-start | bytes 3670016 | tf_op jit(solution)/shard_map/all_to_all | solution.py:135
  513.7 32.7 %all-to-all-done.9 = bf16[32,2,128,112]{2,1,3,0:T(2,128)(2,1)} async-done(((bf16[32,2,128,112]{2,1,3,0:T(2,128)(2,1)}), bf16[32,2,128,112]{2,1,3,0:T(2,128)(2,1)}, u32[]{:S(2)}, u32[]{:S(2)}) %all-to-all-start.9) | async-done | bytes 1835040 | tf_op jit(solution)/shard_map/all_to_all | solution.py:135
  (107 shorter events, 54.2 us)
Async XLA Ops:
  24.4 12.7 %copy-start.11 = (bf16[8,448]{1,0:T(8,128)(2,1)S(1)}, bf16[8,448]{1,0:T(8,128)(2,1)}, u32[]{:S(2)}) copy-start(bf16[8,448]{1,0:T(8,128)(2,1)} %param.15) | copy-start | bytes 21508
  25.5 37.3 %all-to-all-start = ((bf16[32,1,4,3584]{3,2,1,0:T(4,128)(2,1)}), bf16[32,1,4,3584]{3,2,1,0:T(4,128)(2,1)S(1)}, u32[]{:S(2)}, u32[]{:S(2)}) async-start(bf16[32,1,4,3584]{3,2,1,0:T(4,128)(2,1)} %bitcast.5), calls=%async_computation | async-start | bytes 1835008 | tf_op jit(solution)/shard_map/all_to_all | solution.py:76
  50.0 1.2 copy-start.12
  51.5 16.8 %copy-start.8 = (bf16[1536,112]{0,1:T(8,128)(2,1)S(1)}, bf16[1536,112]{0,1:T(8,128)(2,1)}, u32[]{:S(2)}) copy-start(bf16[1536,112]{0,1:T(8,128)(2,1)} %param.18) | copy-start | bytes 1032196
  62.8 7.0 %copy-start.4 = (bf16[32,1,4,3584]{3,2,1,0:T(4,128)(2,1)}, bf16[32,1,4,3584]{3,2,1,0:T(4,128)(2,1)S(1)}, u32[]{:S(2)}) copy-start(bf16[32,1,4,3584]{3,2,1,0:T(4,128)(2,1)S(1)} %all-to-all-done) | copy-start | bytes 2752516
  62.8 29.9 %all-to-all-start.5 = ((bf16[32,1,4,3584]{3,2,1,0:T(4,128)(2,1)}), bf16[32,1,4,3584]{3,2,1,0:T(4,128)(2,1)S(1)}, u32[]{:S(2)}, u32[]{:S(2)}) async-start(bf16[32,1,4,3584]{3,2,1,0:T(4,128)(2,1)} %bitcast.23), calls=%async_computation.5 | async-start | bytes 1835008 | tf_op jit(solution)/shard_map/all_to_all | solution.py:77
  72.2 27.0 %copy-start.9 = (bf16[112,1536]{1,0:T(8,128)(2,1)S(1)}, bf16[112,1536]{1,0:T(8,128)(2,1)}, u32[]{:S(2)}) copy-start(bf16[112,1536]{1,0:T(8,128)(2,1)} %param.16) | copy-start | bytes 1032196
  92.7 0.9 copy-start.5
  93.6 48.9 %all-to-all-start.3 = ((bf16[32,2,128,112]{2,3,1,0:T(8,128)(2,1)}), bf16[32,2,128,112]{2,3,1,0:T(8,128)(2,1)S(1)}, u32[]{:S(2)}, u32[]{:S(2)}) async-start(bf16[32,2,128,112]{2,3,1,0:T(8,128)(2,1)} %broadcast_select_fusion.2), calls=%async_computation.3 | async-start | bytes 3670016 | tf_op jit(solution)/shard_map/all_to_all | solution.py:42
  99.6 2.1 copy-start.10
  142.5 1.2 copy-start.2
  192.9 47.3 %all-to-all-start.2 = ((bf16[32,112,2,128]{3,2,1,0:T(2,128)(2,1)}), bf16[32,112,2,128]{3,2,1,0:T(2,128)(2,1)}, u32[]{:S(2)}, u32[]{:S(2)}) async-start(bf16[32,112,2,128]{3,2,1,0:T(2,128)(2,1)} %get-tuple-element.33), calls=%async_computation.2 | async-start | bytes 3670016 | tf_op jit(solution)/shard_map/all_to_all | solution.py:41
  198.0 141.3 %reduce-scatter.7.cloned.1.call-start = ((), (), s32[]{:S(2)}) async-start(), calls=%async_computation.12 | async-start | bytes 1032192
  240.2 2.1 copy-start.3
  240.2 2.3 copy-start.6
  257.2 110.5 %reduce-scatter.9.cloned.1.call-start = ((), (), s32[]{:S(2)}) async-start(), calls=%async_computation.13 | async-start | bytes 1032192
  341.4 41.1 %all-to-all-start.4 = ((bf16[32,1,4,448]{3,2,1,0:T(4,128)(2,1)}), bf16[32,1,4,448]{3,2,1,0:T(4,128)(2,1)S(1)}, u32[]{:S(2)}, u32[]{:S(2)}) async-start(bf16[32,1,4,448]{3,2,1,0:T(4,128)(2,1)} %copy.106), calls=%async_computation.4 | async-start | bytes 262144 | tf_op jit(solution)/shard_map/all_to_all | solution.py:109
  382.5 20.2 %all-to-all-start.6 = ((bf16[32,1,4,448]{3,2,1,0:T(4,128)(2,1)}), bf16[32,1,4,448]{3,2,1,0:T(4,128)(2,1)S(1)}, u32[]{:S(2)}, u32[]{:S(2)}) async-start(bf16[32,1,4,448]{3,2,1,0:T(4,128)(2,1)} %bitcast.24), calls=%async_computation.6 | async-start | bytes 262144 | tf_op jit(solution)/shard_map/all_to_all | solution.py:112
  402.7 47.4 %all-to-all-start.7 = ((bf16[32,112,2,128]{3,2,1,0:T(2,128)(2,1)}), bf16[32,112,2,128]{3,2,1,0:T(2,128)(2,1)S(1)}, u32[]{:S(2)}, u32[]{:S(2)}) async-start(bf16[32,112,2,128]{3,2,1,0:T(2,128)(2,1)} %reshape.151), calls=%async_computation.7 | async-start | bytes 3670016 | tf_op jit(solution)/shard_map/all_to_all | solution.py:133
  413.2 43.5 %copy-start.7 = (bf16[128,3584]{1,0:T(8,128)(2,1)S(1)}, bf16[128,3584]{1,0:T(8,128)(2,1)}, u32[]{:S(2)}) copy-start(bf16[128,3584]{1,0:T(8,128)(2,1)} %reshape_squeeze.7) | copy-start | bytes 2752516
  450.1 1.3 copy-start
  451.4 47.4 %all-to-all-start.8 = ((bf16[32,112,2,128]{3,2,1,0:T(2,128)(2,1)}), bf16[32,112,2,128]{3,2,1,0:T(2,128)(2,1)}, u32[]{:S(2)}, u32[]{:S(2)}) async-start(bf16[32,112,2,128]{3,2,1,0:T(2,128)(2,1)} %reshape.153), calls=%async_computation.8 | async-start | bytes 3670016 | tf_op jit(solution)/shard_map/all_to_all | solution.py:134
  498.8 47.6 %all-to-all-start.9 = ((bf16[32,2,128,112]{2,1,3,0:T(2,128)(2,1)}), bf16[32,2,128,112]{2,1,3,0:T(2,128)(2,1)}, u32[]{:S(2)}, u32[]{:S(2)}) async-start(bf16[32,2,128,112]{2,1,3,0:T(2,128)(2,1)} %bitcast.119), calls=%async_computation.9 | async-start | bytes 3670016 | tf_op jit(solution)/shard_map/all_to_all | solution.py:135
  505.0 3.0 copy-start.1
Sparse Core Ops, SparseCore 0:
  257.3 27.9 reduce-scatter.6
  339.4 28.1 reduce-scatter.8
where the time goes:
time: 566 us; the launch traced here: 557 us
  waiting for transfers between devices  226 us (40%)
  local copies, waits for them, and re-layouts  151 us (27%)
  blocking collectives  74.9 us (13%)
  starting transfers between devices  59.2 us (10%)
  matrix products  18.5 us (3%)
  between operations  14.5 us (3%)
  other arithmetic  12.7 us (2%)
    unnamed x41, local copies, waits for them, and re-layouts  114 us
    all_to_all x1, blocking collectives, shards(): lax.all_to_all(gate_send, 'expert', split_axis=0, concat_axis=0, tiled=True)  49.1 us
    all_to_all x1, waiting for transfers between devices, shards(): lax.all_to_all(gate_back, 'expert', split_axis=0, concat_axis=0, tiled=True)  36.9 us
    all_to_all x1, waiting for transfers between devices, shards(): lax.all_to_all(up_send, 'expert', split_axis=0, concat_axis=0, tiled=True)  33.3 us
    all_to_all x1, waiting for transfers between devices, shards(): lax.all_to_all(up_back, 'expert', split_axis=0, concat_axis=0, tiled=True)  33 us
    all_to_all x1, waiting for transfers between devices, shards(): lax.all_to_all(down_back, 'expert', split_axis=0, concat_axis=0, tiled=True)  32.7 us
    all_to_all x1, waiting for transfers between devices, shards(): lax.all_to_all(down_send, 'expert', split_axis=0, concat_axis=0, tiled=True)  30.8 us
    all_to_all x1, waiting for transfers between devices, shards(): lax.all_to_all(cotan_slots, 'expert', split_axis=0, concat_axis=0, tiled=...  20.5 us
  transfers between devices with their start and end apart: 11, of which 9 were waited for; matrix products, arithmetic and copies ran while one was open for 27% of the time, Pallas kernels for 0%

commit v1 on v0

v1 whole, which is shorter than its diff:
```python
import jax
import jax.numpy as jnp
from jax import lax
from jax.sharding import PartitionSpec as P

BLK = 128


def contract(left, right, left_dim, right_dim):
    return lax.dot_general(
        left, right, (((left_dim,), (right_dim,)), ((), ())), preferred_element_type=jnp.float32
    )


def shards(tokens, d_out, gate_dense, up_dense, down_dense, block_map, routes, route_gates):
    dp_count = lax.axis_size("dp")
    ex_count = lax.axis_size("expert")
    dp_index = lax.axis_index("dp")
    experts_all = block_map.shape[0]
    per_group = block_map.shape[1] // dp_count
    width = gate_dense.shape[1]
    blocks = width // BLK
    rows_owned = gate_dense.shape[0]
    tok = routes.shape[0]
    owned_map = lax.dynamic_slice_in_dim(block_map, dp_index * per_group, per_group, 1)
    picks = owned_map - dp_index * blocks
    takes = jnp.sum((picks[:, :, None] == jnp.arange(blocks)[None, None, :]).astype(jnp.float32), axis=1)
    named = (routes[:, :, None] == jnp.arange(experts_all)[None, None, :]).astype(jnp.float32)
    named = jnp.sum(named * route_gates[None, :, None], axis=1)
    weight = jnp.sum(named[:, :, None] * takes[None, :, :], axis=1)
    weight = jnp.repeat(weight, BLK, axis=1)

    both = jnp.concatenate([tokens, d_out], axis=0)
    full = lax.all_gather(both, "dp", axis=1, tiled=True)
    full = full.reshape(2, tok, ex_count, rows_owned).transpose(2, 0, 1, 3)
    cols = lax.all_to_all(full, "expert", split_axis=0, concat_axis=0, tiled=True)
    x = cols[:, 0].reshape(ex_count * tok, rows_owned)
    dy = cols[:, 1].reshape(ex_count * tok, rows_owned)
    part = jnp.concatenate(
        [contract(x, gate_dense, 1, 0), contract(x, up_dense, 1, 0), contract(dy, down_dense, 1, 1)], axis=1
    ).astype(jnp.bfloat16)
    sums = lax.psum_scatter(part, "expert", scatter_dimension=0, tiled=True).astype(jnp.float32)
    gate_pre, up_pre, hidden_grad = sums[:, :width], sums[:, width : 2 * width], sums[:, 2 * width :]
    sigma = jax.nn.sigmoid(gate_pre)
    silu = gate_pre * sigma
    hidden = weight * silu * up_pre
    gate_grad = weight * hidden_grad * up_pre * sigma * (1.0 + gate_pre * (1.0 - sigma))
    up_grad = weight * hidden_grad * silu
    mine = jnp.concatenate([gate_grad, up_grad, hidden], axis=1).astype(jnp.bfloat16)
    every = lax.all_gather(mine, "expert", axis=0, tiled=True)
    gate_grad, up_grad, hidden = every[:, :width], every[:, width : 2 * width], every[:, 2 * width :]
    gate_dense_grad = contract(x, gate_grad, 0, 0)
    up_dense_grad = contract(x, up_grad, 0, 0)
    down_dense_grad = contract(hidden, dy, 0, 0)
    out_part = contract(hidden, down_dense, 1, 0).astype(jnp.bfloat16)
    in_part = (contract(gate_grad, gate_dense, 1, 1) + contract(up_grad, up_dense, 1, 1)).astype(jnp.bfloat16)
    pair = jnp.stack([out_part.reshape(ex_count, tok, rows_owned), in_part.reshape(ex_count, tok, rows_owned)], axis=1)
    back = lax.all_to_all(pair, "expert", split_axis=0, concat_axis=0, tiled=True)
    back = back.transpose(1, 2, 0, 3).reshape(2 * tok, ex_count * rows_owned)
    done = lax.psum_scatter(back, "dp", scatter_dimension=1, tiled=True)
    return (done[:tok], done[tok:], gate_dense_grad, up_dense_grad, down_dense_grad)


def solution(mesh):
    in_specs = (
        P("expert", "dp"),
        P("expert", "dp"),
        P("expert", "dp"),
        P("expert", "dp"),
        P("dp", "expert"),
        P(),
        P("expert", None),
        P(),
    )
    out_specs = (
        P("expert", "dp"),
        P("expert", "dp"),
        P("expert", "dp"),
        P("expert", "dp"),
        P("dp", "expert"),
    )
    return jax.shard_map(shards, mesh=mesh, in_specs=in_specs, out_specs=out_specs, check_vma=False)
```

time: 566 us -> 401 us (0.71); the launches traced: 557 us -> 398 us
  local copies, waits for them, and re-layouts: 151 us -> 6.13 us
  waiting for transfers between devices: 226 us -> 322 us
  starting transfers between devices: 59.2 us -> 5.96 us
  blocking collectives: 74.9 us -> 35 us
  matrix products: 18.5 us -> 9.62 us
  other arithmetic: 12.7 us -> 4.96 us
    reduce_scatter x0 -> x1, waiting for transfers between devices: none -> 211 us  [shards(): lax.psum_scatter(part, 'expert', scatter_dimension=0, tiled=True)]
    all_to_all x9 -> x1, waiting for transfers between devices: 206 us -> 8.17 us  [shards(): lax.all_to_all(pair, 'expert', split_axis=0, concat_axis=0, tiled=True)]
    unnamed x41 -> x16, local copies, waits for them, and re-layouts: 114 us -> 2.79 us
    all_gather x0 -> x1, waiting for transfers between devices: none -> 78 us  [shards(): every = lax.all_gather(mine, 'expert', axis=0, tiled=True)]
    all_to_all x9 -> x1, starting transfers between devices: 59 us -> 5.84 us  [shards(): lax.all_to_all(pair, 'expert', split_axis=0, concat_axis=0, tiled=True)]
    all_to_all x1, blocking collectives: 49.1 us -> 22.2 us  [shards(): lax.all_to_all(full, 'expert', split_axis=0, concat_axis=0, tiled=True)]
    reshape x11 -> x2, local copies, waits for them, and re-layouts: 16.2 us -> 0.39 us  [the longest x1 0.2 us: shards(): back = back.transpose(1, 2, 0, 3).reshape(2 * tok, ex_count * rows_owned)]
    all_gather x2 -> x1, blocking collectives: 25.8 us -> 12.8 us  [shards(): full = lax.all_gather(both, 'dp', axis=1, tiled=True)]
  transfers between devices with their start and end apart: 11 -> 4, of which waited for: 9 -> 4; matrix products, arithmetic and copies ran while one was open for 27% -> 1% of each run, Pallas kernels for 0% -> 0%
where the time goes in v1:
time: 401 us; the launch traced here: 398 us
  waiting for transfers between devices  322 us (80%)
  blocking collectives  35 us (9%)
  between operations  13.9 us (3%)
  matrix products  9.62 us (2%)
  local copies, waits for them, and re-layouts  6.13 us (2%)
  starting transfers between devices  5.96 us (1%)
  other arithmetic  4.96 us (1%)
    reduce_scatter x1, waiting for transfers between devices, shards(): lax.psum_scatter(part, 'expert', scatter_dimension=0, tiled=True)  211 us
    all_gather x1, waiting for transfers between devices, shards(): every = lax.all_gather(mine, 'expert', axis=0, tiled=True)  78 us
    unnamed x4, waiting for transfers between devices  25 us
    all_to_all x1, blocking collectives, shards(): lax.all_to_all(full, 'expert', split_axis=0, concat_axis=0, tiled=True)  22.2 us
    all_gather x1, blocking collectives, shards(): full = lax.all_gather(both, 'dp', axis=1, tiled=True)  12.8 us
    dot_general x9, matrix products, contract(): lax.dot_general(left, right, (((left_dim,), (right_dim,)), ((), ())), pre...  9.62 us
    all_to_all x1, waiting for transfers between devices, shards(): lax.all_to_all(pair, 'expert', split_axis=0, concat_axis=0, tiled=True)  8.17 us
  transfers between devices with their start and end apart: 4, of which 4 were waited for; matrix products, arithmetic and copies ran while one was open for 1% of the time, Pallas kernels for 0%

profile of v1, /device:TPU:2, one launch (start us, length us, event | category | flops | bytes accessed | tf_op | source)
XLA Modules:
  0.0 397.7 jit_solution(18264860661240629594)
XLA Ops:
  7.2 0.8 maximum_bitcast_fusion
  8.0 12.8 %all-gather = bf16[8,448,16]{1,2,0:T(8,128)(2,1)S(1)} all-gather(bf16[1,448,16]{1,2,0:T(8,128)(2,1)S(1)} %maximum_bitcast_fusion), channel_id=1, replica_groups=mesh['dp'=8,'expert'=32] {'dp'}, dimensions={0}, use_global_device_ids=true | all-gather | bytes 129024 | tf_op jit(solution)/shard_map/all_gather | solution.py:34
  20.9 0.2 reshape.28
  21.1 0.2 reshape.25
  21.3 22.2 %all_to_all.10 = bf16[32,2,8,112]{3,2,1,0:T(8,128)(2,1)S(1)} all-to-all(bf16[32,2,8,112]{3,2,1,0:T(8,128)(2,1)S(1)} %copy.36), channel_id=1, replica_groups=mesh['dp'=8,'expert'=32] {'expert'}, dimensions={0} | all-to-all | bytes 229376 | tf_op jit(solution)/shard_map/all_to_all | solution.py:36
  43.5 1.3 convolution_convert_fusion
  44.9 0.3 convolution_convert_fusion.1
  45.2 0.3 convolution_convert_fusion.2
  45.6 1.6 pad_maximum_fusion
  47.3 0.7 dynamic-slice_subtract_fusion
  48.2 210.9 %reduce-scatter.5.cloned.1.call-done = bf16[8,4608]{1,0:T(8,128)(2,1)} async-done(((bf16[256,4608]{1,0:T(8,128)(2,1)}), bf16[8,4608]{1,0:T(8,128)(2,1)}) %reduce-scatter.5.cloned.1.call-update) | async-done | bytes 73744 | tf_op jit(solution)/shard_map/reduce_scatter | solution.py:42
  259.1 0.9 convert_element_type.16
  260.0 0.1 multiply_convert_fusion.1
  260.1 0.6 pad_maximum_fusion.2
  260.8 78.0 %all-gather.3.cloned.1.call-done = bf16[256,4608]{1,0:T(8,128)(2,1)} async-done(((bf16[8,4608]{1,0:T(8,128)(2,1)}), bf16[256,4608]{1,0:T(8,128)(2,1)}) %all-gather.3.cloned.1.call-update) | async-done | bytes 2359312 | tf_op jit(solution)/shard_map/all_gather | solution.py:50
  338.8 1.7 fusion.6
  340.5 2.1 fusion
  342.6 0.9 copy.38
  343.6 0.4 convolution_convert_fusion.3
  343.9 0.1 copy.37
  344.1 0.7 copy.39
  344.8 5.8 %all-to-all-start.1 = ((bf16[32,2,8,112]{3,2,1,0:T(8,128)(2,1)}), bf16[32,2,8,112]{3,2,1,0:T(8,128)(2,1)S(1)}, u32[]{:S(2)}, u32[]{:S(2)}) async-start(bf16[32,2,8,112]{3,2,1,0:T(8,128)(2,1)} %copy.39), calls=%async_computation.2 | async-start | bytes 262144 | tf_op jit(solution)/shard_map/all_to_all | solution.py:58
  350.7 1.1 fusion.1
  351.8 1.1 fusion.4
  353.0 8.2 %all-to-all-done.1 = bf16[32,2,8,112]{3,2,1,0:T(8,128)(2,1)S(1)} async-done(((bf16[32,2,8,112]{3,2,1,0:T(8,128)(2,1)}), bf16[32,2,8,112]{3,2,1,0:T(8,128)(2,1)S(1)}, u32[]{:S(2)}, u32[]{:S(2)}) %all-to-all-start.1) | async-done | bytes 114720 | tf_op jit(solution)/shard_map/all_to_all | solution.py:58
  361.2 0.2 reshape.26
  361.4 1.2 copy.41
  362.6 1.2 fusion.8
  363.8 25.0 %reduce-scatter.7.cloned.1.call-done = bf16[448,16]{1,0:T(8,128)(2,1)} async-done(((bf16[3584,16]{1,0:T(8,128)(2,1)}), bf16[448,16]{1,0:T(8,128)(2,1)}) %reduce-scatter.7.cloned.1.call-update) | async-done | bytes 14352
  388.7 1.1 fusion.15
  389.8 0.7 copy.43
  390.5 0.7 copy.44
  (25 shorter events, 0.6 us)
Async XLA Ops:
  7.2 38.1 %copy-start = (bf16[112,1536]{1,0:T(8,128)(2,1)S(1)}, bf16[112,1536]{1,0:T(8,128)(2,1)}, u32[]{:S(2)}) copy-start(bf16[112,1536]{1,0:T(8,128)(2,1)} %param.10) | copy-start | bytes 1032196
  7.2 37.7 %copy-start.2 = (bf16[112,1536]{1,0:T(8,128)(2,1)S(1)}, bf16[112,1536]{1,0:T(8,128)(2,1)}, u32[]{:S(2)}) copy-start(bf16[112,1536]{1,0:T(8,128)(2,1)} %param.11) | copy-start | bytes 1032196
  7.2 251.9 %reduce-scatter.5.cloned.1.call-start = ((), (), s32[]{:S(2)}) async-start(), calls=%async_computation.4 | async-start | bytes 2433024 | tf_op jit(solution)/shard_map/reduce_scatter | solution.py:42
  47.2 0.9 copy-start.4
  47.2 0.9 copy-start.5
  47.2 296.3 %copy-start.3 = (bf16[1536,112]{0,1:T(8,128)(2,1)S(1)}, bf16[1536,112]{0,1:T(8,128)(2,1)}, u32[]{:S(2)}) copy-start(bf16[1536,112]{0,1:T(8,128)(2,1)} %param.12) | copy-start | bytes 1032196
  47.2 291.6 %all-gather.3.cloned.1.call-start = ((), (), s32[]{:S(2)}) async-start(), calls=%async_computation.5 | async-start | bytes 2433024 | tf_op jit(solution)/shard_map/all_gather | solution.py:50
  338.8 4.8 %copy-start.1 = (bf16[256,4608]{1,0:T(8,128)(2,1)S(1)}, bf16[256,4608]{1,0:T(8,128)(2,1)}, u32[]{:S(2)}) copy-start(bf16[256,4608]{1,0:T(8,128)(2,1)} %all-gather.3.cloned.1.call-done) | copy-start | bytes 7077892
  344.8 16.3 %all-to-all-start.1 = ((bf16[32,2,8,112]{3,2,1,0:T(8,128)(2,1)}), bf16[32,2,8,112]{3,2,1,0:T(8,128)(2,1)S(1)}, u32[]{:S(2)}, u32[]{:S(2)}) async-start(bf16[32,2,8,112]{3,2,1,0:T(8,128)(2,1)} %copy.39), calls=%async_computation.2 | async-start | bytes 262144 | tf_op jit(solution)/shard_map/all_to_all | solution.py:58
  350.6 38.1 %reduce-scatter.7.cloned.1.call-start = ((), (), s32[]{:S(2)}) async-start(), calls=%async_computation.6 | async-start | bytes 1032192
Sparse Core Ops, SparseCore 0:
  47.3 211.7 reduce-scatter.4
  262.3 76.5 all-gather.2
  362.8 25.9 reduce-scatter.6

commit v2 on v1

v2 whole, which is shorter than its diff:
```python
import functools

import jax
import jax.numpy as jnp
from jax import lax
from jax.experimental import pallas as pl
from jax.experimental.pallas import tpu as pltpu
from jax.sharding import PartitionSpec as P

BLK = 128
MESH = pl.DeviceIdType.MESH


def contract(left, right, left_dim, right_dim):
    return lax.dot_general(
        left, right, (((left_dim,), (right_dim,)), ((), ())), preferred_element_type=jnp.float32
    )


def kernel(
    nj, ny, nc,
    tok_ref, cot_ref, gate_ref, up_ref, down_ref, wt_ref,
    mixed_ref, dtok_ref, gate_out, up_out, down_out,
    xs, xt, xb, wbuf, wgu, wd, wdf, rs_send, rs_recv, ag, gu_send, d_send, acc, op_send, op_recv, t_send, t_recv,
    xt_ss, xt_rs, wt_ss, wt_rs, xb_ss, xb_rs, w_ss, w_rs, r_ss, r_rs, a_ss, a_rs, g_ss, g_rs, o_ss, o_rs, t_ss, t_rs,
):
    nz = nj
    j = lax.axis_index("dp")
    e = lax.axis_index("expert")
    z, y = e // ny, lax.rem(e, ny)
    rows = gate_ref.shape[0]
    quarter = gate_ref.shape[1] // ny
    group = 8 * ny

    def at_y(k):
        return (j, z * ny + k)

    def at_z(k):
        return (j, k * ny + y)

    def at_j(k):
        return (k, e)

    def at_t(k):
        return (z, j * ny + k)

    def others(n, me, body):
        def step(i, _):
            body(lax.rem(me + i, n))
            return 0

        lax.fori_loop(1, n, step, 0)

    def crossing(body, own):
        def step(k, _):
            same = jnp.logical_and(z == j, k == y)

            @pl.when(jnp.logical_not(same))
            def _():
                body(k)

            if own is not None:
                @pl.when(same)
                def _():
                    own(k)

            return 0

        lax.fori_loop(0, ny, step, 0)

    def remote(src, dst, ss, rs, device):
        return pltpu.make_async_remote_copy(
            src_ref=src, dst_ref=dst, send_sem=ss, recv_sem=rs, device_id=device, device_id_type=MESH
        )

    barrier = pltpu.get_barrier_semaphore()

    def greet(device):
        pl.semaphore_signal(barrier, inc=1, device_id=device, device_id_type=MESH)

    others(ny, y, lambda k: greet(at_y(k)))
    others(nz, z, lambda k: greet(at_z(k)))
    others(nj, j, lambda k: greet(at_j(k)))
    count = (ny - 1) + (nz - 1) + (nj - 1)

    @pl.when(z != j)
    def _():
        def step(k, _):
            greet(at_t(k))
            return 0

        lax.fori_loop(0, ny, step, 0)
        pl.semaphore_wait(barrier, count + ny)

    @pl.when(z == j)
    def _():
        pl.semaphore_wait(barrier, count)

    xs[...] = jnp.concatenate(
        [tok_ref[...].astype(jnp.float32), cot_ref[...].astype(jnp.float32)], axis=0
    ).astype(jnp.bfloat16)

    def x_copy(k):
        return remote(xs, xt.at[y], xt_ss.at[k], xt_rs.at[y], at_t(k))

    def x_wait(k):
        return remote(xs, xt.at[k], xt_ss.at[k], xt_rs.at[k], at_t(k))

    def x_own(k):
        xt[k] = xs[...]

    crossing(lambda k: x_copy(k).start(), x_own)

    def wt_copy(k):
        return remote(wt_ref.at[k], wbuf.at[y], wt_ss.at[k], wt_rs.at[y], at_y(k))

    def wt_wait(k):
        return remote(wt_ref.at[k], wbuf.at[k], wt_ss.at[k], wt_rs.at[k], at_y(k))

    others(ny, y, lambda k: wt_copy(k).start())
    wbuf[y] = wt_ref[y]

    def columns(k, c):
        return pl.ds(pl.multiple_of(k * quarter + c * BLK, BLK), BLK)

    def band(k):
        return pl.ds(pl.multiple_of(k * rows, 16), rows)

    def w_copies(k, c, slot):
        return (
            remote(gate_ref.at[:, columns(k, c)], wgu.at[c, band(slot), pl.ds(0, BLK)],
                   w_ss.at[c, 0, k], w_rs.at[c, 0, slot], at_y(k)),
            remote(up_ref.at[:, columns(k, c)], wgu.at[c, band(slot), pl.ds(BLK, BLK)],
                   w_ss.at[c, 1, k], w_rs.at[c, 1, slot], at_y(k)),
            remote(down_ref.at[columns(k, c), :], wd.at[c, slot],
                   w_ss.at[c, 2, k], w_rs.at[c, 2, slot], at_y(k)),
        )

    def start_all(copies):
        for copy in copies:
            copy.start()

    def recv_all(copies):
        for copy in copies:
            copy.wait_recv()

    def send_all(copies):
        for copy in copies:
            copy.wait_send()

    for c in range(nc):
        others(ny, y, lambda k: start_all(w_copies(k, c, y)))
    for c in range(nc):
        wgu[c, band(y), 0:BLK] = gate_ref[:, columns(y, c)]
        wgu[c, band(y), BLK : 2 * BLK] = up_ref[:, columns(y, c)]
        wd[c, y] = down_ref[columns(y, c), :]

    crossing(lambda k: x_wait(k).wait_recv(), None)
    landed = xt[...].astype(jnp.float32)
    xb[j, 0] = landed[:, :8].reshape(group, -1).astype(jnp.bfloat16)
    xb[j, 1] = landed[:, 8:].reshape(group, -1).astype(jnp.bfloat16)

    def xb_copy(k, slot):
        return remote(xb.at[slot], xb.at[slot], xb_ss.at[k], xb_rs.at[slot], at_j(k))

    others(nj, j, lambda k: xb_copy(k, j).start())
    others(nj, j, lambda k: xb_copy(k, k).wait_recv())
    tokens_all = nj * group
    feats = xb.shape[3]
    x = xb[:, 0].reshape(tokens_all, feats)
    dy = xb[:, 1].reshape(tokens_all, feats)

    def rs_copy(k, c, slot):
        return remote(rs_send.at[c, k], rs_recv.at[c, slot], r_ss.at[c, k], r_rs.at[c, slot], at_z(k))

    for c in range(nc):
        others(ny, y, lambda k: recv_all(w_copies(k, c, k)))
        wdf[c] = jnp.concatenate([wd[c, k] for k in range(ny)], axis=1)
        pre = contract(x, wgu[c], 1, 0)
        hid = contract(dy, wdf[c], 1, 1)
        rs_send[c, :, :, 0 : 2 * BLK] = pre.reshape(nz, group, 2 * BLK).astype(jnp.bfloat16)
        rs_send[c, :, :, 2 * BLK : 3 * BLK] = hid.reshape(nz, group, BLK).astype(jnp.bfloat16)
        others(nz, z, lambda k: rs_copy(k, c, z).start())
        rs_recv[c, z] = rs_send[c, z]

    others(ny, y, lambda k: wt_wait(k).wait_recv())

    def ag_copy(k, c, slot):
        return remote(ag.at[c, slot], ag.at[c, slot], a_ss.at[c, k], a_rs.at[c, slot], at_z(k))

    for c in range(nc):
        others(nz, z, lambda k: rs_copy(k, c, k).wait_recv())
        total = jnp.sum(rs_recv[c].astype(jnp.float32), axis=0)
        gate_pre, up_pre, hidden_grad = total[:, :BLK], total[:, BLK : 2 * BLK], total[:, 2 * BLK :]
        weight = wbuf[:, :, c * BLK : (c + 1) * BLK].reshape(group, BLK)
        sigma = jax.nn.sigmoid(gate_pre)
        silu = gate_pre * sigma
        scaled = weight * hidden_grad
        ag[c, z, :, 0:BLK] = (scaled * up_pre * sigma * (1.0 + gate_pre * (1.0 - sigma))).astype(jnp.bfloat16)
        ag[c, z, :, BLK : 2 * BLK] = (scaled * silu).astype(jnp.bfloat16)
        ag[c, z, :, 2 * BLK : 3 * BLK] = (weight * silu * up_pre).astype(jnp.bfloat16)
        others(nz, z, lambda k: ag_copy(k, c, z).start())

    def g_copies(k, c, slot):
        return (
            remote(gu_send.at[c, band(k), pl.ds(0, BLK)], gate_out.at[:, columns(slot, c)],
                   g_ss.at[c, 0, k], g_rs.at[c, 0, slot], at_y(k)),
            remote(gu_send.at[c, band(k), pl.ds(BLK, BLK)], up_out.at[:, columns(slot, c)],
                   g_ss.at[c, 1, k], g_rs.at[c, 1, slot], at_y(k)),
            remote(d_send.at[c, k], down_out.at[columns(slot, c), :],
                   g_ss.at[c, 2, k], g_rs.at[c, 2, slot], at_y(k)),
        )

    for c in range(nc):
        others(nz, z, lambda k: ag_copy(k, c, k).wait_recv())
        pair = ag[c, :, :, 0 : 2 * BLK].reshape(tokens_all, 2 * BLK)
        hidden = ag[c, :, :, 2 * BLK : 3 * BLK].reshape(tokens_all, BLK)
        gu_send[c] = contract(x, pair, 0, 0).astype(jnp.bfloat16)
        down_part = contract(hidden, dy, 0, 0).astype(jnp.bfloat16)
        for k in range(ny):
            d_send[c, k] = down_part[:, k * rows : (k + 1) * rows]
        others(ny, y, lambda k: start_all(g_copies(k, c, y)))
        out_part = contract(hidden, wdf[c], 1, 0)
        in_part = contract(pair, wgu[c], 1, 1)
        if c == 0:
            acc[0], acc[1] = out_part, in_part
        else:
            acc[0] += out_part
            acc[1] += in_part
    op_send[:, 0] = acc[0].reshape(nj, group, feats).astype(jnp.bfloat16)
    op_send[:, 1] = acc[1].reshape(nj, group, feats).astype(jnp.bfloat16)

    def op_copy(k, slot):
        return remote(op_send.at[k], op_recv.at[slot], o_ss.at[k], o_rs.at[slot], at_j(k))

    others(nj, j, lambda k: op_copy(k, j).start())
    op_recv[j] = op_send[j]
    for c in range(nc):
        gate_out[:, columns(y, c)] = gu_send[c, band(y), 0:BLK]
        up_out[:, columns(y, c)] = gu_send[c, band(y), BLK : 2 * BLK]
        down_out[columns(y, c), :] = d_send[c, y]
    others(nj, j, lambda k: op_copy(k, k).wait_recv())
    summed = jnp.sum(op_recv[...].astype(jnp.float32), axis=0).reshape(2, ny, 8, feats)
    t_send[...] = jnp.concatenate([summed[0], summed[1]], axis=1).astype(jnp.bfloat16)

    def t_copy(k):
        return remote(t_send.at[k], t_recv.at[y], t_ss.at[k], t_rs.at[y], at_t(k))

    def t_wait(k):
        return remote(t_send.at[k], t_recv.at[k], t_ss.at[k], t_rs.at[k], at_t(k))

    def t_own(k):
        t_recv[k] = t_send[k]

    crossing(lambda k: t_copy(k).start(), t_own)
    crossing(lambda k: t_wait(k).wait_recv(), None)
    final = jnp.sum(t_recv[...].astype(jnp.float32), axis=0)
    mixed_ref[...] = final[:8].astype(jnp.bfloat16)
    dtok_ref[...] = final[8:].astype(jnp.bfloat16)

    for c in range(nc):
        others(ny, y, lambda k: recv_all(g_copies(k, c, k)))
    crossing(lambda k: x_copy(k).wait_send(), None)
    crossing(lambda k: t_copy(k).wait_send(), None)
    others(ny, y, lambda k: wt_copy(k).wait_send())
    others(nj, j, lambda k: xb_copy(k, j).wait_send())
    others(nj, j, lambda k: op_copy(k, j).wait_send())
    for c in range(nc):
        others(ny, y, lambda k: send_all(w_copies(k, c, y)))
        others(nz, z, lambda k: rs_copy(k, c, z).wait_send())
        others(nz, z, lambda k: ag_copy(k, c, z).wait_send())
        others(ny, y, lambda k: send_all(g_copies(k, c, y)))


def shards(tokens, d_out, gate_dense, up_dense, down_dense, block_map, routes, route_gates):
    nj = lax.axis_size("dp")
    ny = lax.axis_size("expert") // nj
    dp_index = lax.axis_index("dp")
    experts_all = block_map.shape[0]
    per_group = block_map.shape[1] // nj
    rows, width = gate_dense.shape
    blocks = width // BLK
    tok, feats = tokens.shape
    nc = blocks // ny
    group = tok * ny
    owned_map = lax.dynamic_slice_in_dim(block_map, dp_index * per_group, per_group, 1)
    picks = owned_map - dp_index * blocks
    takes = jnp.sum((picks[:, :, None] == jnp.arange(blocks)[None, None, :]).astype(jnp.float32), axis=1)
    named = (routes[:, :, None] == jnp.arange(experts_all)[None, None, :]).astype(jnp.float32)
    named = jnp.sum(named * route_gates[None, :, None], axis=1)
    weight = jnp.sum(named[:, :, None] * takes[None, :, :], axis=1)
    weight = weight.reshape(tok, ny, nc).transpose(1, 0, 2)
    weight = jnp.broadcast_to(weight[:, :, :, None], (ny, tok, nc, BLK)).reshape(ny, tok, nc * BLK)

    half, full = jnp.bfloat16, jnp.float32
    dma = pltpu.SemaphoreType.DMA
    vmem = pl.BlockSpec(memory_space=pltpu.VMEM)
    mixed, d_tokens, gate_grad, up_grad, down_grad = pl.pallas_call(
        functools.partial(kernel, nj, ny, nc),
        out_shape=(
            jax.ShapeDtypeStruct((tok, feats), half),
            jax.ShapeDtypeStruct((tok, feats), half),
            jax.ShapeDtypeStruct((rows, width), half),
            jax.ShapeDtypeStruct((rows, width), half),
            jax.ShapeDtypeStruct((width, rows), half),
        ),
        in_specs=[vmem] * 6,
        out_specs=(vmem,) * 5,
        scratch_shapes=[
            pltpu.VMEM((2 * tok, feats), half),
            pltpu.VMEM((ny, 2 * tok, feats), half),
            pltpu.VMEM((nj, 2, group, feats), half),
            pltpu.VMEM((ny, tok, nc * BLK), full),
            pltpu.VMEM((nc, ny * rows, 2 * BLK), half),
            pltpu.VMEM((nc, ny, BLK, rows), half),
            pltpu.VMEM((nc, BLK, ny * rows), half),
            pltpu.VMEM((nc, nj, group, 3 * BLK), half),
            pltpu.VMEM((nc, nj, group, 3 * BLK), half),
            pltpu.VMEM((nc, nj, group, 3 * BLK), half),
            pltpu.VMEM((nc, ny * rows, 2 * BLK), half),
            pltpu.VMEM((nc, ny, BLK, rows), half),
            pltpu.VMEM((2, nj * group, feats), full),
            pltpu.VMEM((nj, 2, group, feats), half),
            pltpu.VMEM((nj, 2, group, feats), half),
            pltpu.VMEM((ny, 2 * tok, feats), half),
            pltpu.VMEM((ny, 2 * tok, feats), half),
            dma((ny,)), dma((ny,)), dma((ny,)), dma((ny,)),
            dma((nj,)), dma((nj,)),
            dma((nc, 3, ny)), dma((nc, 3, ny)),
            dma((nc, nj)), dma((nc, nj)), dma((nc, nj)), dma((nc, nj)),
            dma((nc, 3, ny)), dma((nc, 3, ny)),
            dma((nj,)), dma((nj,)), dma((ny,)), dma((ny,)),
        ],
        compiler_params=pltpu.CompilerParams(
            collective_id=0, has_side_effects=True, vmem_limit_bytes=40 * 1024 * 1024
        ),
    )(tokens, d_out, gate_dense, up_dense, down_dense, weight)
    return (
        mixed,
        d_tokens,
        gate_grad.astype(jnp.float32),
        up_grad.astype(jnp.float32),
        down_grad.astype(jnp.float32),
    )


def solution(mesh):
    in_specs = (
        P("expert", "dp"),
        P("expert", "dp"),
        P("expert", "dp"),
        P("expert", "dp"),
        P("dp", "expert"),
        P(),
        P("expert", None),
        P(),
    )
    out_specs = (
        P("expert", "dp"),
        P("expert", "dp"),
        P("expert", "dp"),
        P("expert", "dp"),
        P("dp", "expert"),
    )
    return jax.shard_map(shards, mesh=mesh, in_specs=in_specs, out_specs=out_specs, check_vma=False)
```

time: 401 us -> 80.7 us (0.20)
  waiting for transfers between devices: 322 us -> 0 us
  Pallas kernels: 0 us -> 72.2 us
  blocking collectives: 35 us -> 0 us
  between operations: 13.9 us -> 0.74 us
  matrix products: 9.62 us -> 0 us
  starting transfers between devices: 5.96 us -> 0 us
    reduce_scatter x1 -> x0, waiting for transfers between devices: 211 us -> none  [shards(): lax.psum_scatter(part, 'expert', scatter_dimension=0, tiled=True)]
    all_gather x1 -> x0, waiting for transfers between devices: 78 us -> none  [shards(): every = lax.all_gather(mine, 'expert', axis=0, tiled=True)]
    pallas_call x0 -> x1, Pallas kernels: none -> 72.2 us  [shards(): pl.pallas_call(functools.partial(kernel, nj, ny, nc), out_shape=(jax.Shap...]
    unnamed x4 -> x0, waiting for transfers between devices: 25 us -> none
    all_to_all x1 -> x0, blocking collectives: 22.2 us -> none  [shards(): lax.all_to_all(full, 'expert', split_axis=0, concat_axis=0, tiled=True)]
    all_gather x1 -> x0, blocking collectives: 12.8 us -> none  [shards(): full = lax.all_gather(both, 'dp', axis=1, tiled=True)]
    dot_general x9 -> x0, matrix products: 9.62 us -> none  [contract(): lax.dot_general(left, right, (((left_dim,), (right_dim,)), ((), ())), pre...]
    all_to_all x1 -> x0, waiting for transfers between devices: 8.17 us -> none  [shards(): lax.all_to_all(pair, 'expert', split_axis=0, concat_axis=0, tiled=True)]
  transfers between devices with their start and end apart: 4 -> 0, of which waited for: 4 -> 0; matrix products, arithmetic and copies ran while one was open for 1% -> 0% of each run, Pallas kernels for 0% -> 0%
where the time goes in v2:
time: 80.7 us; the launch traced here: 79.3 us
  Pallas kernels  72.2 us (89%)
  local copies, waits for them, and re-layouts  3.6 us (4%)
  other arithmetic  2.73 us (3%)
    pallas_call x1, Pallas kernels, shards(): pl.pallas_call(functools.partial(kernel, nj, ny, nc), out_shape=(jax.Shap...  72.2 us
    unnamed x16, local copies, waits for them, and re-layouts  3.51 us

profile of v2, /device:TPU:2, one launch (start us, length us, event | category | flops | bytes accessed | tf_op | source)
XLA Modules:
  0.0 79.3 jit_solution(8072611947599911555)
XLA Ops:
  0.6 0.0 copy-start.4
  0.6 0.0 copy-start.5
  0.7 0.7 dynamic-slice_subtract_fusion
  1.4 0.0 copy-done.4
  1.4 0.0 copy-done.5
  1.4 0.1 select_reduce_fusion
  1.5 0.1 multiply_reduce_fusion
  1.6 0.1 broadcast_bitcast_fusion.wt_ref
  1.7 0.0 copy-start
  1.7 0.0 copy-start.1
  1.7 0.0 copy-start.2
  1.7 0.0 copy-start.3
  1.7 1.3 %copy.19.down_ref = bf16[1536,112]{1,0:T(8,128)(2,1)S(1)} copy(bf16[1536,112]{0,1:T(8,128)(2,1)} %param.12) | data formatting | bytes 688128 | tf_op args[4]
  3.0 0.0 copy-done
  3.0 0.0 copy-done.1
  3.0 0.0 copy-done.2
  3.0 0.0 copy-done.3
  3.0 72.2 %shard_map.119 = (bf16[8,448]{1,0:T(8,128)(2,1)S(1)}, bf16[8,448]{1,0:T(8,128)(2,1)S(1)}, bf16[112,1536]{1,0:T(8,128)(2,1)S(1)}, bf16[112,1536]{1,0:T(8,128)(2,1)S(1)}, bf16[1536,112]{1,0:T(8,128)(2,1)S(1)}) custom-call(bf16[8,448]{1,0:T(8,128)(2,1)S(1)} %copy-done.2, bf16[8,448]{1,0:T(8,128)(2,1)S(1)} %copy-done.3, bf16[112,1536]{1,0:T(8,128)(2,1)S(1)} %copy-done, ...), custom_call_target="tpu_custom_call" | custom-call | tf_op jit(solution)/shard_map/pallas_call | solution.py:298
  75.2 0.9 %convert_element_type.14 = f32[112,1536]{1,0:T(8,128)} convert(bf16[112,1536]{1,0:T(8,128)(2,1)S(1)} %get-tuple-element.12) | non-fusion elementwise | flops 172032 | bytes 1032192 | tf_op jit(solution)/shard_map/convert_element_type | solution.py:341
  76.2 0.9 %convert_element_type.15 = f32[112,1536]{1,0:T(8,128)} convert(bf16[112,1536]{1,0:T(8,128)(2,1)S(1)} %get-tuple-element.13) | non-fusion elementwise | flops 172032 | bytes 1032192 | tf_op jit(solution)/shard_map/convert_element_type | solution.py:342
  77.1 1.0 %copy.20 = f32[1536,112]{0,1:T(8,128)} copy(bf16[1536,112]{1,0:T(8,128)(2,1)S(1)} %get-tuple-element.14) | data formatting | bytes 1032192
  78.1 0.6 copy.23
  78.7 0.6 copy.24
  (2 shorter events, 0.0 us)
Async XLA Ops:
  0.6 0.7 copy-start.4
  0.6 0.7 copy-start.5
  1.7 1.3 %copy-start = (bf16[112,1536]{1,0:T(8,128)(2,1)S(1)}, bf16[112,1536]{1,0:T(8,128)(2,1)}, u32[]{:S(2)}) copy-start(bf16[112,1536]{1,0:T(8,128)(2,1)} %gate_ref.1) | copy-start | bytes 1032196
  1.7 1.3 %copy-start.1 = (bf16[112,1536]{1,0:T(8,128)(2,1)S(1)}, bf16[112,1536]{1,0:T(8,128)(2,1)}, u32[]{:S(2)}) copy-start(bf16[112,1536]{1,0:T(8,128)(2,1)} %up_ref.1) | copy-start | bytes 1032196
  1.7 1.3 %copy-start.2 = (bf16[8,448]{1,0:T(8,128)(2,1)S(1)}, bf16[8,448]{1,0:T(8,128)(2,1)}, u32[]{:S(2)}) copy-start(bf16[8,448]{1,0:T(8,128)(2,1)} %tok_ref.1) | copy-start | bytes 21508
  1.7 1.3 %copy-start.3 = (bf16[8,448]{1,0:T(8,128)(2,1)S(1)}, bf16[8,448]{1,0:T(8,128)(2,1)}, u32[]{:S(2)}) copy-start(bf16[8,448]{1,0:T(8,128)(2,1)} %cot_ref.1) | copy-start | bytes 21508

commit v3 on v2

--- a/solution.py
+++ b/solution.py
@@ -21,7 +21,7 @@
     nj, ny, nc,
     tok_ref, cot_ref, gate_ref, up_ref, down_ref, wt_ref,
     mixed_ref, dtok_ref, gate_out, up_out, down_out,
-    xs, xt, xb, wbuf, wgu, wd, wdf, rs_send, rs_recv, ag, gu_send, d_send, acc, op_send, op_recv, t_send, t_recv,
+    xs, xt, xb, wbuf, wall, rs_send, rs_recv, ag, grads, acc, op_send, op_recv, t_send, t_recv,
     xt_ss, xt_rs, wt_ss, wt_rs, xb_ss, xb_rs, w_ss, w_rs, r_ss, r_rs, a_ss, a_rs, g_ss, g_rs, o_ss, o_rs, t_ss, t_rs,
 ):
     nz = nj
@@ -128,11 +128,11 @@
 
     def w_copies(k, c, slot):
         return (
-            remote(gate_ref.at[:, columns(k, c)], wgu.at[c, band(slot), pl.ds(0, BLK)],
+            remote(gate_ref.at[:, columns(k, c)], wall.at[c, band(slot), pl.ds(0, BLK)],
                    w_ss.at[c, 0, k], w_rs.at[c, 0, slot], at_y(k)),
-            remote(up_ref.at[:, columns(k, c)], wgu.at[c, band(slot), pl.ds(BLK, BLK)],
+            remote(up_ref.at[:, columns(k, c)], wall.at[c, band(slot), pl.ds(BLK, BLK)],
                    w_ss.at[c, 1, k], w_rs.at[c, 1, slot], at_y(k)),
-            remote(down_ref.at[columns(k, c), :], wd.at[c, slot],
+            remote(down_ref.at[:, columns(k, c)], wall.at[c, band(slot), pl.ds(2 * BLK, BLK)],
                    w_ss.at[c, 2, k], w_rs.at[c, 2, slot], at_y(k)),
         )
 
@@ -151,9 +151,9 @@
     for c in range(nc):
         others(ny, y, lambda k: start_all(w_copies(k, c, y)))
     for c in range(nc):
-        wgu[c, band(y), 0:BLK] = gate_ref[:, columns(y, c)]
-        wgu[c, band(y), BLK : 2 * BLK] = up_ref[:, columns(y, c)]
-        wd[c, y] = down_ref[columns(y, c), :]
+        wall[c, band(y), 0:BLK] = gate_ref[:, columns(y, c)]
+        wall[c, band(y), BLK : 2 * BLK] = up_ref[:, columns(y, c)]
+        wall[c, band(y), 2 * BLK : 3 * BLK] = down_ref[:, columns(y, c)]
 
     crossing(lambda k: x_wait(k).wait_recv(), None)
     landed = xt[...].astype(jnp.float32)
@@ -175,9 +175,8 @@
 
     for c in range(nc):
         others(ny, y, lambda k: recv_all(w_copies(k, c, k)))
-        wdf[c] = jnp.concatenate([wd[c, k] for k in range(ny)], axis=1)
-        pre = contract(x, wgu[c], 1, 0)
-        hid = contract(dy, wdf[c], 1, 1)
+        pre = contract(x, wall[c, :, 0 : 2 * BLK], 1, 0)
+        hid = contract(dy, wall[c, :, 2 * BLK : 3 * BLK], 1, 0)
         rs_send[c, :, :, 0 : 2 * BLK] = pre.reshape(nz, group, 2 * BLK).astype(jnp.bfloat16)
         rs_send[c, :, :, 2 * BLK : 3 * BLK] = hid.reshape(nz, group, BLK).astype(jnp.bfloat16)
         others(nz, z, lambda k: rs_copy(k, c, z).start())
@@ -203,11 +202,11 @@
 
     def g_copies(k, c, slot):
         return (
-            remote(gu_send.at[c, band(k), pl.ds(0, BLK)], gate_out.at[:, columns(slot, c)],
+            remote(grads.at[c, band(k), pl.ds(0, BLK)], gate_out.at[:, columns(slot, c)],
                    g_ss.at[c, 0, k], g_rs.at[c, 0, slot], at_y(k)),
-            remote(gu_send.at[c, band(k), pl.ds(BLK, BLK)], up_out.at[:, columns(slot, c)],
+            remote(grads.at[c, band(k), pl.ds(BLK, BLK)], up_out.at[:, columns(slot, c)],
                    g_ss.at[c, 1, k], g_rs.at[c, 1, slot], at_y(k)),
-            remote(d_send.at[c, k], down_out.at[columns(slot, c), :],
+            remote(grads.at[c, band(k), pl.ds(2 * BLK, BLK)], down_out.at[:, columns(slot, c)],
                    g_ss.at[c, 2, k], g_rs.at[c, 2, slot], at_y(k)),
         )
 
@@ -215,13 +214,11 @@
         others(nz, z, lambda k: ag_copy(k, c, k).wait_recv())
         pair = ag[c, :, :, 0 : 2 * BLK].reshape(tokens_all, 2 * BLK)
         hidden = ag[c, :, :, 2 * BLK : 3 * BLK].reshape(tokens_all, BLK)
-        gu_send[c] = contract(x, pair, 0, 0).astype(jnp.bfloat16)
-        down_part = contract(hidden, dy, 0, 0).astype(jnp.bfloat16)
-        for k in range(ny):
-            d_send[c, k] = down_part[:, k * rows : (k + 1) * rows]
+        grads[c, :, 0 : 2 * BLK] = contract(x, pair, 0, 0).astype(jnp.bfloat16)
+        grads[c, :, 2 * BLK : 3 * BLK] = contract(dy, hidden, 0, 0).astype(jnp.bfloat16)
         others(ny, y, lambda k: start_all(g_copies(k, c, y)))
-        out_part = contract(hidden, wdf[c], 1, 0)
-        in_part = contract(pair, wgu[c], 1, 1)
+        out_part = contract(hidden, wall[c, :, 2 * BLK : 3 * BLK], 1, 1)
+        in_part = contract(pair, wall[c, :, 0 : 2 * BLK], 1, 1)
         if c == 0:
             acc[0], acc[1] = out_part, in_part
         else:
@@ -236,9 +233,9 @@
     others(nj, j, lambda k: op_copy(k, j).start())
     op_recv[j] = op_send[j]
     for c in range(nc):
-        gate_out[:, columns(y, c)] = gu_send[c, band(y), 0:BLK]
-        up_out[:, columns(y, c)] = gu_send[c, band(y), BLK : 2 * BLK]
-        down_out[columns(y, c), :] = d_send[c, y]
+        gate_out[:, columns(y, c)] = grads[c, band(y), 0:BLK]
+        up_out[:, columns(y, c)] = grads[c, band(y), BLK : 2 * BLK]
+        down_out[:, columns(y, c)] = grads[c, band(y), 2 * BLK : 3 * BLK]
     others(nj, j, lambda k: op_copy(k, k).wait_recv())
     summed = jnp.sum(op_recv[...].astype(jnp.float32), axis=0).reshape(2, ny, 8, feats)
     t_send[...] = jnp.concatenate([summed[0], summed[1]], axis=1).astype(jnp.bfloat16)
@@ -302,7 +299,7 @@
             jax.ShapeDtypeStruct((tok, feats), half),
             jax.ShapeDtypeStruct((rows, width), half),
             jax.ShapeDtypeStruct((rows, width), half),
-            jax.ShapeDtypeStruct((width, rows), half),
+            jax.ShapeDtypeStruct((rows, width), half),
         ),
         in_specs=[vmem] * 6,
         out_specs=(vmem,) * 5,
@@ -311,14 +308,11 @@
             pltpu.VMEM((ny, 2 * tok, feats), half),
             pltpu.VMEM((nj, 2, group, feats), half),
             pltpu.VMEM((ny, tok, nc * BLK), full),
-            pltpu.VMEM((nc, ny * rows, 2 * BLK), half),
-            pltpu.VMEM((nc, ny, BLK, rows), half),
-            pltpu.VMEM((nc, BLK, ny * rows), half),
+            pltpu.VMEM((nc, ny * rows, 3 * BLK), half),
             pltpu.VMEM((nc, nj, group, 3 * BLK), half),
             pltpu.VMEM((nc, nj, group, 3 * BLK), half),
             pltpu.VMEM((nc, nj, group, 3 * BLK), half),
-            pltpu.VMEM((nc, ny * rows, 2 * BLK), half),
-            pltpu.VMEM((nc, ny, BLK, rows), half),
+            pltpu.VMEM((nc, ny * rows, 3 * BLK), half),
             pltpu.VMEM((2, nj * group, feats), full),
             pltpu.VMEM((nj, 2, group, feats), half),
             pltpu.VMEM((nj, 2, group, feats), half),
@@ -334,13 +328,13 @@
         compiler_params=pltpu.CompilerParams(
             collective_id=0, has_side_effects=True, vmem_limit_bytes=40 * 1024 * 1024
         ),
-    )(tokens, d_out, gate_dense, up_dense, down_dense, weight)
+    )(tokens, d_out, gate_dense, up_dense, down_dense.T, weight)
     return (
         mixed,
         d_tokens,
         gate_grad.astype(jnp.float32),
         up_grad.astype(jnp.float32),
-        down_grad.astype(jnp.float32),
+        down_grad.astype(jnp.float32).T,
     )
 
 

time: 80.7 us -> 83.4 us (1.033); the launches traced: 79.3 us -> 83.1 us
  local copies, waits for them, and re-layouts: 3.6 us -> 5.5 us
  Pallas kernels: 72.2 us -> 73.3 us
  other arithmetic: 2.73 us -> 3.63 us
    unnamed x16, local copies, waits for them, and re-layouts: 3.51 us -> 5.41 us
    pallas_call x1, Pallas kernels: 72.2 us -> 73.3 us  [shards(): pl.pallas_call(functools.partial(kernel, nj, ny, nc), out_shape=(jax.Shap...]
    transpose x0 -> x1, other arithmetic: none -> 0.91 us  [shards(): down_grad.astype(jnp.float32)]
where the time goes in v3:
time: 83.4 us; the launch traced here: 83.1 us
  Pallas kernels  73.3 us (88%)
  local copies, waits for them, and re-layouts  5.5 us (7%)
  other arithmetic  3.63 us (4%)
    pallas_call x1, Pallas kernels, shards(): pl.pallas_call(functools.partial(kernel, nj, ny, nc), out_shape=(jax.Shap...  73.3 us
    unnamed x16, local copies, waits for them, and re-layouts  5.41 us

profile of v3, /device:TPU:2, one launch (start us, length us, event | category | flops | bytes accessed | tf_op | source)
XLA Modules:
  0.0 83.1 jit_solution(1257619117240411608)
XLA Ops:
  0.6 0.0 copy-start.5
  0.6 0.7 dynamic-slice_subtract_fusion
  1.3 0.0 copy-start.6
  1.3 0.0 copy-done.5
  1.4 0.7 copy-done.6
  2.0 0.1 select_reduce_fusion
  2.1 0.1 multiply_reduce_fusion
  2.2 0.0 copy-start.3
  2.2 0.0 copy-start.4
  2.3 0.1 broadcast_bitcast_fusion.wt_ref
  2.3 0.6 copy-done.3
  2.9 0.0 copy-done.4
  2.9 0.0 copy-start
  2.9 1.0 %copy-done = bf16[112,1536]{1,0:T(8,128)(2,1)S(1)} copy-done((bf16[112,1536]{1,0:T(8,128)(2,1)S(1)}, bf16[112,1536]{1,0:T(8,128)(2,1)}, u32[]{:S(2)}) %copy-start) | copy-done | bytes 344088
  3.9 0.0 copy-start.1
  3.9 1.0 %copy-done.1 = bf16[112,1536]{1,0:T(8,128)(2,1)S(1)} copy-done((bf16[112,1536]{1,0:T(8,128)(2,1)S(1)}, bf16[112,1536]{1,0:T(8,128)(2,1)}, u32[]{:S(2)}) %copy-start.1) | copy-done | bytes 344088
  4.9 0.0 copy-start.2
  4.9 1.0 %copy-done.2 = bf16[1536,112]{0,1:T(8,128)(2,1)S(1)} copy-done((bf16[1536,112]{0,1:T(8,128)(2,1)S(1)}, bf16[1536,112]{0,1:T(8,128)(2,1)}, u32[]{:S(2)}) %copy-start.2) | copy-done | bytes 344088
  5.9 73.3 %shard_map.119 = (bf16[8,448]{1,0:T(8,128)(2,1)S(1)}, bf16[8,448]{1,0:T(8,128)(2,1)S(1)}, bf16[112,1536]{1,0:T(8,128)(2,1)S(1)}, bf16[112,1536]{1,0:T(8,128)(2,1)S(1)}, bf16[112,1536]{1,0:T(8,128)(2,1)S(1)}) custom-call(bf16[8,448]{1,0:T(8,128)(2,1)S(1)} %copy-done.3, bf16[8,448]{1,0:T(8,128)(2,1)S(1)} %copy-done.4, bf16[112,1536]{1,0:T(8,128)(2,1)S(1)} %copy-done, ...), custom_call_target="tpu_custom_call" | custom-call | tf_op jit(solution)/shard_map/pallas_call | solution.py:295
  79.2 0.9 %convert_element_type.12 = f32[112,1536]{1,0:T(8,128)} convert(bf16[112,1536]{1,0:T(8,128)(2,1)S(1)} %get-tuple-element.12) | non-fusion elementwise | flops 172032 | bytes 1032192 | tf_op jit(solution)/shard_map/convert_element_type | solution.py:335
  80.1 0.9 %convert_element_type.13 = f32[112,1536]{1,0:T(8,128)} convert(bf16[112,1536]{1,0:T(8,128)(2,1)S(1)} %get-tuple-element.13) | non-fusion elementwise | flops 172032 | bytes 1032192 | tf_op jit(solution)/shard_map/convert_element_type | solution.py:336
  81.0 0.9 %convert_bitcast_fusion = f32[1536,112]{0,1:T(8,128)} fusion(bf16[112,1536]{1,0:T(8,128)(2,1)S(1)} %get-tuple-element.14), kind=kLoop, calls=%fused_computation | loop fusion | flops 172032 | bytes 1032192 | tf_op jit(solution)/shard_map/transpose | solution.py:337
  81.9 0.6 copy.17
  82.5 0.6 copy.18
  (2 shorter events, 0.0 us)
Async XLA Ops:
  0.6 0.7 copy-start.5
  1.3 0.7 copy-start.6
  2.2 0.7 copy-start.3
  2.2 0.7 copy-start.4
  2.9 1.0 %copy-start = (bf16[112,1536]{1,0:T(8,128)(2,1)S(1)}, bf16[112,1536]{1,0:T(8,128)(2,1)}, u32[]{:S(2)}) copy-start(bf16[112,1536]{1,0:T(8,128)(2,1)} %gate_ref.1) | copy-start | bytes 1032196
  3.9 1.0 %copy-start.1 = (bf16[112,1536]{1,0:T(8,128)(2,1)S(1)}, bf16[112,1536]{1,0:T(8,128)(2,1)}, u32[]{:S(2)}) copy-start(bf16[112,1536]{1,0:T(8,128)(2,1)} %up_ref.1) | copy-start | bytes 1032196
  4.9 1.0 %copy-start.2 = (bf16[1536,112]{0,1:T(8,128)(2,1)S(1)}, bf16[1536,112]{0,1:T(8,128)(2,1)}, u32[]{:S(2)}) copy-start(bf16[1536,112]{0,1:T(8,128)(2,1)} %param.12) | copy-start | bytes 1032196

commit v4 on v3

v4 whole, which is shorter than its diff:
```python
import functools

import jax
import jax.numpy as jnp
from jax import lax
from jax.experimental import pallas as pl
from jax.experimental.pallas import tpu as pltpu
from jax.sharding import PartitionSpec as P

BLK = 128
MESH = pl.DeviceIdType.MESH
HALF, FULL = jnp.bfloat16, jnp.float32


def contract(left, right, left_dim, right_dim):
    return lax.dot_general(left, right, (((left_dim,), (right_dim,)), ((), ())), preferred_element_type=FULL)


def widen(rows, lanes):
    fill = jnp.zeros(rows.shape[:-1] + (lanes - rows.shape[-1],), rows.dtype)
    return jnp.concatenate([rows, fill], axis=-1).astype(HALF)


def kernel(
    nj, ny, nc, per,
    tok_ref, cot_ref, routes_ref, map_ref, gates_ref, gate_ref, up_ref, down_ref,
    mixed_ref, dtok_ref, gate_out, up_out, down_out,
    xs, xt, xb, dyb, xtr, dytr, wts, wbuf, wall, part, rs_buf, rs_recv, ag, grads, acc,
    op_send, op_core, op_buf, op_recv, t_send, t_recv,
    xt_ss, xt_rs, xb_ss, xb_rs, xc_ss, wt_ss, wt_rs, wl_s, w_ss, w_rs, r_ss, r_rs, a_ss, a_rs, g_ss, g_rs,
    oc_ss, oc_rs, o_ss, o_rs, t_ss, t_rs,
):
    nz, nx = nj, nj // 2
    hops_down, hops_up = nz // 2, nz - 1 - nz // 2
    j = lax.axis_index("dp")
    e = lax.axis_index("expert")
    x_me, core = j // 2, lax.rem(j, 2)
    z, y = e // ny, lax.rem(e, ny)
    rows = gate_ref.shape[0]
    quarter = gate_ref.shape[1] // ny
    feats, padded = tok_ref.shape[1], xs.shape[1]
    group = 8 * ny
    tokens_all = nj * group

    def at_y(k):
        return (j, z * ny + k)

    def at_z(k):
        return (j, lax.rem(z + k + nz, nz) * ny + y)

    def at_x(k):
        return (2 * k + core, e)

    def at_t(k):
        return (z, j * ny + k)

    other_core = (2 * x_me + 1 - core, e)

    def others(n, me, body):
        def step(i, _):
            body(lax.rem(me + i, n))
            return 0

        lax.fori_loop(1, n, step, 0)

    def crossing(body, own):
        def step(k, _):
            same = jnp.logical_and(z == j, k == y)

            @pl.when(jnp.logical_not(same))
            def _():
                body(k)

            if own is not None:
                @pl.when(same)
                def _():
                    own(k)

            return 0

        lax.fori_loop(0, ny, step, 0)

    def remote(src, dst, ss, rs, device):
        return pltpu.make_async_remote_copy(
            src_ref=src, dst_ref=dst, send_sem=ss, recv_sem=rs, device_id=device, device_id_type=MESH
        )

    barrier = pltpu.get_barrier_semaphore()

    def greet(device):
        pl.semaphore_signal(barrier, inc=1, device_id=device, device_id_type=MESH)

    others(ny, y, lambda k: greet(at_y(k)))
    greet(at_z(1))
    greet(at_z(-1))
    others(nx, x_me, lambda k: greet(at_x(k)))
    greet(other_core)
    count = (ny - 1) + 2 + (nx - 1) + 1

    @pl.when(z != j)
    def _():
        def step(k, _):
            greet(at_t(k))
            return 0

        lax.fori_loop(0, ny, step, 0)

    xs[...] = widen(jnp.concatenate([tok_ref[...].astype(FULL), cot_ref[...].astype(FULL)], axis=0), padded)

    @pl.when(z != j)
    def _():
        pl.semaphore_wait(barrier, count + ny)

    @pl.when(z == j)
    def _():
        pl.semaphore_wait(barrier, count)

    def x_copy(k):
        return remote(xs, xt.at[y], xt_ss.at[k], xt_rs.at[y], at_t(k))

    def x_wait(k):
        return remote(xs, xt.at[k], xt_ss.at[k], xt_rs.at[k], at_t(k))

    def x_own(k):
        xt[k] = xs[...]

    crossing(lambda k: x_copy(k).start(), x_own)

    def columns(k, c):
        return pl.ds(pl.multiple_of(k * quarter + c * BLK, BLK), BLK)

    def band(k):
        return pl.ds(pl.multiple_of(k * rows, 16), rows)

    def w_copies(k, c, slot):
        return [
            remote(ref.at[:, columns(k, c)], wall.at[c, band(slot), pl.ds(i * BLK, BLK)],
                   w_ss.at[c, i, k], w_rs.at[c, i, slot], at_y(k))
            for i, ref in enumerate((gate_ref, up_ref, down_ref))
        ]

    def w_local(c):
        return [
            pltpu.make_async_copy(ref.at[:, columns(y, c)], wall.at[c, band(y), pl.ds(i * BLK, BLK)], wl_s.at[c, i])
            for i, ref in enumerate((gate_ref, up_ref, down_ref))
        ]

    def start_all(copies):
        for copy in copies:
            copy.start()

    def wait_all(copies):
        for copy in copies:
            copy.wait()

    def recv_all(copies):
        for copy in copies:
            copy.wait_recv()

    def send_all(copies):
        for copy in copies:
            copy.wait_send()

    others(ny, y, lambda k: start_all(w_copies(k, 0, y)))

    crossing(lambda k: x_wait(k).wait_recv(), None)
    landed = xt[...].astype(FULL)[:, :, :feats]
    xb[j] = jnp.concatenate(
        [landed[:, :8].reshape(group, feats), landed[:, 8:].reshape(group, feats)], axis=1
    ).astype(HALF)

    def xb_copy(k, slot):
        return remote(xb.at[slot], xb.at[slot], xb_ss.at[k], xb_rs.at[slot], at_x(k))

    def xc_copy(k, side):
        slot = 2 * k + side
        return remote(xb.at[slot], xb.at[slot], xc_ss.at[k], xb_rs.at[slot], other_core)

    others(nx, x_me, lambda k: xb_copy(k, j).start())
    xc_copy(x_me, core).start()
    for c in range(1, nc):
        others(ny, y, lambda k: start_all(w_copies(k, c, y)))
    for c in range(nc):
        start_all(w_local(c))

    experts = map_ref.shape[1]
    names = lax.broadcasted_iota(jnp.int32, (8, experts), 1)
    named = jnp.zeros((8, experts), FULL)
    for k in range(routes_ref.shape[1]):
        named = named + jnp.where(routes_ref[:, k : k + 1] == names, gates_ref[k], 0.0)
    picks = [map_ref[pl.ds(j * per + q, 1), :] - j * (ny * nc) for q in range(per)]
    for k in range(ny):
        for c in range(nc):
            takes = sum((pick == k * nc + c).astype(FULL) for pick in picks)
            weight = jnp.sum(named * takes, axis=1, keepdims=True)
            wts[k, :, c * BLK : (c + 1) * BLK] = jnp.broadcast_to(weight, (8, BLK))

    def wt_copy(k):
        return remote(wts.at[k], wbuf.at[y], wt_ss.at[k], wt_rs.at[y], at_y(k))

    def wt_wait(k):
        return remote(wts.at[k], wbuf.at[k], wt_ss.at[k], wt_rs.at[k], at_y(k))

    others(ny, y, lambda k: wt_copy(k).start())
    wbuf[y] = wts[y]

    def forward(k):
        xb_copy(k, 2 * k + core).wait_recv()
        xc_copy(k, core).start()

    others(nx, x_me, forward)

    def from_core(k, _):
        xc_copy(k, 1 - core).wait_recv()
        return 0

    lax.fori_loop(0, nx, from_core, 0)
    dyb[...] = xb[:, :, feats:].reshape(tokens_all, feats)

    def x_all():
        return xb[:, :, :feats].reshape(tokens_all, feats)

    def lane(down, s):
        return s - 1 if down else hops_down + s - 1

    def rs_copy(c, down, s):
        i = lane(down, s)
        return remote(rs_buf.at[c, i], rs_recv.at[c, i], r_ss.at[c, i], r_rs.at[c, i], at_z(-1 if down else 1))

    def rs_send(c, down, s):
        t = lax.rem(z - (hops_down - s + 1) + nz, nz) if down else lax.rem(z + (hops_up - s + 1), nz)
        value = part[c, t]
        if s > 1:
            value = value + rs_recv[c, lane(down, s - 1)].astype(FULL)
        rs_buf[c, lane(down, s)] = value.astype(HALF)
        rs_copy(c, down, s).start()

    def ag_copy(c, down, s, arriving):
        i = lane(not down, s)
        shift = s if arriving else s - 1
        slot = lax.rem(z + shift, nz) if down else lax.rem(z - shift + nz, nz)
        return remote(ag.at[c, slot], ag.at[c, slot], a_ss.at[c, i], a_rs.at[c, i], at_z(-1 if down else 1))

    def g_copies(k, c, slot):
        return [
            remote(grads.at[c, band(k), pl.ds(i * BLK, BLK)], ref.at[:, columns(slot, c)],
                   g_ss.at[c, i, k], g_rs.at[c, i, slot], at_y(k))
            for i, ref in enumerate((gate_out, up_out, down_out))
        ]

    def first(c):
        wait_all(w_local(c))
        others(ny, y, lambda k: recv_all(w_copies(k, c, k)))
        part[c, :, :, 0 : 2 * BLK] = contract(x_all(), wall[c, :, 0 : 2 * BLK], 1, 0).reshape(nz, group, 2 * BLK)
        part[c, :, :, 2 * BLK : 3 * BLK] = contract(dyb[...], wall[c, :, 2 * BLK : 3 * BLK], 1, 0).reshape(nz, group, BLK)
        rs_send(c, True, 1)
        if hops_up:
            rs_send(c, False, 1)

    def middle(c):
        if c == 0:
            others(ny, y, lambda k: wt_wait(k).wait_recv())
        total = part[c, z] + rs_recv[c, lane(True, hops_down)].astype(FULL)
        if hops_up:
            total = total + rs_recv[c, lane(False, hops_up)].astype(FULL)
        gate_pre, up_pre, hidden_grad = total[:, :BLK], total[:, BLK : 2 * BLK], total[:, 2 * BLK :]
        weight = wbuf[:, :, c * BLK : (c + 1) * BLK].reshape(group, BLK)
        sigma = jax.nn.sigmoid(gate_pre)
        silu = gate_pre * sigma
        scaled = weight * hidden_grad
        ag[c, z, :, 0:BLK] = (scaled * up_pre * sigma * (1.0 + gate_pre * (1.0 - sigma))).astype(HALF)
        ag[c, z, :, BLK : 2 * BLK] = (scaled * silu).astype(HALF)
        ag[c, z, :, 2 * BLK : 3 * BLK] = (weight * silu * up_pre).astype(HALF)
        ag_copy(c, False, 1, False).start()
        if hops_up:
            ag_copy(c, True, 1, False).start()

    def last(c):
        pair = ag[c, :, :, 0 : 2 * BLK].reshape(tokens_all, 2 * BLK)
        hidden = ag[c, :, :, 2 * BLK : 3 * BLK].reshape(tokens_all, BLK)

        def block_grads():
            grads[c, :, 0 : 2 * BLK] = contract(xtr[...], pair, 1, 0).astype(HALF)
            grads[c, :, 2 * BLK : 3 * BLK] = contract(dytr[...], hidden, 1, 0).astype(HALF)
            others(ny, y, lambda k: start_all(g_copies(k, c, y)))

        if c < nc - 1:
            block_grads()
        out_part = contract(hidden, wall[c, :, 2 * BLK : 3 * BLK], 1, 1)
        in_part = contract(pair, wall[c, :, 0 : 2 * BLK], 1, 1)
        if c > 0:
            out_part = out_part + acc[0]
            in_part = in_part + acc[1]
        if c < nc - 1:
            acc[0], acc[1] = out_part, in_part
        else:
            parts = jnp.concatenate([out_part, in_part], axis=1).reshape(nx, 2, group, 2 * feats)
            op_send[...] = parts.astype(HALF)
            others(nx, x_me, lambda k: oc_copy(k).start())
            oc_copy(x_me).start()
            block_grads()

    def oc_copy(k):
        return remote(op_send.at[k, 1 - core], op_core.at[k], oc_ss.at[k], oc_rs.at[k], other_core)

    def op_copy(k, slot):
        return remote(op_buf.at[k], op_recv.at[slot], o_ss.at[k], o_rs.at[slot], at_x(k))

    def stage(c, s):
        if s == 0:
            first(c)
        elif s <= hops_down:
            rs_copy(c, True, s).wait_recv()
            if s < hops_down:
                rs_send(c, True, s + 1)
            if s <= hops_up:
                rs_copy(c, False, s).wait_recv()
                if s < hops_up:
                    rs_send(c, False, s + 1)
            if s == hops_down:
                middle(c)
        else:
            s = s - hops_down
            ag_copy(c, False, s, True).wait_recv()
            if s < hops_down:
                ag_copy(c, False, s + 1, False).start()
            if s <= hops_up:
                ag_copy(c, True, s, True).wait_recv()
                if s < hops_up:
                    ag_copy(c, True, s + 1, False).start()
            if s == hops_down:
                last(c)

    stages = 2 * hops_down + 1
    for slot in range(stages + nc - 1):
        for c in reversed(range(nc)):
            if 0 <= slot - c < stages:
                stage(c, slot - c)
        if slot == nc - 1:
            xtr[...] = x_all().T
            dytr[...] = dyb[...].T

    def pass_on(k):
        oc_copy(k).wait_recv()
        op_buf[k] = (op_send[k, core].astype(FULL) + op_core[k].astype(FULL)).astype(HALF)
        op_copy(k, x_me).start()

    others(nx, x_me, pass_on)
    oc_copy(x_me).wait_recv()
    for c in range(nc):
        for i, ref in enumerate((gate_out, up_out, down_out)):
            ref[:, columns(y, c)] = grads[c, band(y), i * BLK : (i + 1) * BLK]
    op_recv[x_me] = op_core[x_me]
    others(nx, x_me, lambda k: op_copy(k, k).wait_recv())
    summed = jnp.sum(op_recv[...].astype(FULL), axis=0) + op_send[x_me, core].astype(FULL)
    t_send[...] = widen(
        jnp.concatenate(
            [summed[:, :feats].reshape(ny, 8, feats), summed[:, feats:].reshape(ny, 8, feats)], axis=1
        ),
        padded,
    )

    def t_copy(k):
        return remote(t_send.at[k], t_recv.at[y], t_ss.at[k], t_rs.at[y], at_t(k))

    def t_wait(k):
        return remote(t_send.at[k], t_recv.at[k], t_ss.at[k], t_rs.at[k], at_t(k))

    def t_own(k):
        t_recv[k] = t_send[k]

    crossing(lambda k: t_copy(k).start(), t_own)

    for c in range(nc):
        others(ny, y, lambda k: recv_all(g_copies(k, c, k)))
    crossing(lambda k: x_copy(k).wait_send(), None)
    others(ny, y, lambda k: wt_copy(k).wait_send())
    others(nx, x_me, lambda k: xb_copy(k, j).wait_send())
    for k in range(nx):
        xc_copy(k, core).wait_send()
        oc_copy(k).wait_send()
    others(nx, x_me, lambda k: op_copy(k, x_me).wait_send())
    for c in range(nc):
        others(ny, y, lambda k: send_all(w_copies(k, c, y)))
        for down, hops in ((True, hops_down), (False, hops_up)):
            for s in range(1, hops + 1):
                rs_copy(c, down, s).wait_send()
                ag_copy(c, not down, s, False).wait_send()
        others(ny, y, lambda k: send_all(g_copies(k, c, y)))

    crossing(lambda k: t_wait(k).wait_recv(), None)
    final = jnp.sum(t_recv[...].astype(FULL), axis=0)
    mixed_ref[...] = final[:8, :feats].astype(HALF)
    dtok_ref[...] = final[8:, :feats].astype(HALF)
    crossing(lambda k: t_copy(k).wait_send(), None)


def finish(mixed_ref, dtok_ref, gate_ref, up_ref, down_ref, mixed_out, dtok_out, gate_out, up_out, down_out):
    mixed_out[...] = mixed_ref[...]
    dtok_out[...] = dtok_ref[...]
    for source, target in ((gate_ref, gate_out), (up_ref, up_out), (down_ref, down_out)):
        target[...] = source[...].astype(FULL)


def shards(tokens, d_out, gate_dense, up_dense, down_dense, block_map, routes, route_gates):
    nj = lax.axis_size("dp")
    ny = lax.axis_size("expert") // nj
    nx = nj // 2
    per = block_map.shape[1] // nj
    rows, width = gate_dense.shape
    tok, feats = tokens.shape
    nc = width // BLK // ny
    group = tok * ny
    padded = -(-feats // BLK) * BLK
    hops = nj - 1
    dma = pltpu.SemaphoreType.DMA
    vmem = pl.BlockSpec(memory_space=pltpu.VMEM)
    smem = pl.BlockSpec(memory_space=pltpu.SMEM)
    hbm = pl.BlockSpec(memory_space=pltpu.HBM)
    outs = (
        jax.ShapeDtypeStruct((tok, feats), HALF),
        jax.ShapeDtypeStruct((tok, feats), HALF),
    ) + (jax.ShapeDtypeStruct((rows, width), HALF),) * 3
    results = pl.pallas_call(
        functools.partial(kernel, nj, ny, nc, per),
        out_shape=outs,
        in_specs=[vmem] * 4 + [smem] + [hbm] * 3,
        out_specs=(vmem,) * 5,
        scratch_shapes=[
            pltpu.VMEM((2 * tok, padded), HALF),
            pltpu.VMEM((ny, 2 * tok, padded), HALF),
            pltpu.VMEM((nj, group, 2 * feats), HALF),
            pltpu.VMEM((nj * group, feats), HALF),
            pltpu.VMEM((feats, nj * group), HALF),
            pltpu.VMEM((feats, nj * group), HALF),
            pltpu.VMEM((ny, tok, nc * BLK), FULL),
            pltpu.VMEM((ny, tok, nc * BLK), FULL),
            pltpu.VMEM((nc, ny * rows, 3 * BLK), HALF),
            pltpu.VMEM((nc, nj, group, 3 * BLK), FULL),
            pltpu.VMEM((nc, hops, group, 3 * BLK), HALF),
            pltpu.VMEM((nc, hops, group, 3 * BLK), HALF),
            pltpu.VMEM((nc, nj, group, 3 * BLK), HALF),
            pltpu.VMEM((nc, ny * rows, 3 * BLK), HALF),
            pltpu.VMEM((2, nj * group, feats), FULL),
            pltpu.VMEM((nx, 2, group, 2 * feats), HALF),
            pltpu.VMEM((nx, group, 2 * feats), HALF),
            pltpu.VMEM((nx, group, 2 * feats), HALF),
            pltpu.VMEM((nx, group, 2 * feats), HALF),
            pltpu.VMEM((ny, 2 * tok, padded), HALF),
            pltpu.VMEM((ny, 2 * tok, padded), HALF),
            dma((ny,)), dma((ny,)), dma((nx,)), dma((nj,)), dma((nx,)),
            dma((ny,)), dma((ny,)), dma((nc, 3)),
            dma((nc, 3, ny)), dma((nc, 3, ny)),
            dma((nc, hops)), dma((nc, hops)), dma((nc, hops)), dma((nc, hops)),
            dma((nc, 3, ny)), dma((nc, 3, ny)),
            dma((nx,)), dma((nx,)), dma((nx,)), dma((nx,)), dma((ny,)), dma((ny,)),
        ],
        compiler_params=pltpu.CompilerParams(
            collective_id=0, has_side_effects=True, vmem_limit_bytes=40 * 1024 * 1024
        ),
    )(tokens, d_out, routes, block_map.T, route_gates, gate_dense, up_dense, down_dense.T)
    mixed, d_tokens, gate_grad, up_grad, down_grad = pl.pallas_call(
        finish,
        out_shape=outs[:2] + (jax.ShapeDtypeStruct((rows, width), FULL),) * 3,
        in_specs=[vmem] * 5,
        out_specs=(vmem,) * 5,
        compiler_params=pltpu.CompilerParams(vmem_limit_bytes=16 * 1024 * 1024),
    )(*results)
    return mixed, d_tokens, gate_grad, up_grad, down_grad.T


def solution(mesh):
    in_specs = (
        P("expert", "dp"),
        P("expert", "dp"),
        P("expert", "dp"),
        P("expert", "dp"),
        P("dp", "expert"),
        P(),
        P("expert", None),
        P(),
    )
    out_specs = (
        P("expert", "dp"),
        P("expert", "dp"),
        P("expert", "dp"),
        P("expert", "dp"),
        P("dp", "expert"),
    )
    return jax.shard_map(shards, mesh=mesh, in_specs=in_specs, out_specs=out_specs, check_vma=False)
```

time: 83.4 us -> 78.1 us (0.936)
  the two profiles are of different devices: /device:TPU:2 before, /device:TPU:7 now
where the time goes in v4:
time: 78.1 us; the launch traced here: 77.7 us
  Pallas kernels  70.7 us (91%)
  local copies, waits for them, and re-layouts  6.36 us (8%)
    pallas_call x1, Pallas kernels, shards(): pl.pallas_call(functools.partial(kernel, nj, ny, nc, per), out_shape=outs...  69.3 us
    unnamed x16, local copies, waits for them, and re-layouts  6.36 us

profile of v4, /device:TPU:7, one launch (start us, length us, event | category | flops | bytes accessed | tf_op | source)
XLA Modules:
  0.0 77.7 jit_solution(682582765974786803)
XLA Ops:
  0.6 0.0 copy-start.7
  0.6 0.6 copy-done.7
  1.3 0.0 copy-start
  1.3 1.0 %copy-done = bf16[112,1536]{1,0:T(8,128)(2,1)S(1)} copy-done((bf16[112,1536]{1,0:T(8,128)(2,1)S(1)}, bf16[112,1536]{1,0:T(8,128)(2,1)}, u32[]{:S(2)}) %copy-start) | copy-done | bytes 344088
  2.3 0.0 copy-start.1
  2.3 1.0 %copy-done.1 = bf16[112,1536]{1,0:T(8,128)(2,1)S(1)} copy-done((bf16[112,1536]{1,0:T(8,128)(2,1)S(1)}, bf16[112,1536]{1,0:T(8,128)(2,1)}, u32[]{:S(2)}) %copy-start.1) | copy-done | bytes 344088
  3.2 0.0 copy-start.2
  3.3 1.0 %copy-done.2 = bf16[1536,112]{0,1:T(8,128)(2,1)S(1)} copy-done((bf16[1536,112]{0,1:T(8,128)(2,1)S(1)}, bf16[1536,112]{0,1:T(8,128)(2,1)}, u32[]{:S(2)}) %copy-start.2) | copy-done | bytes 344088
  4.2 0.0 copy-start.3
  4.2 0.7 copy-done.3
  4.9 0.0 copy-start.4
  4.9 0.7 copy-done.4
  5.6 0.0 copy-start.5
  5.6 0.7 copy-done.5
  6.3 0.0 copy-start.6
  6.3 0.7 copy-done.6
  7.0 69.3 %shard_map.119 = (bf16[8,448]{1,0:T(8,128)(2,1)S(1)}, bf16[8,448]{1,0:T(8,128)(2,1)S(1)}, bf16[112,1536]{1,0:T(8,128)(2,1)S(1)}, bf16[112,1536]{1,0:T(8,128)(2,1)S(1)}, bf16[112,1536]{1,0:T(8,128)(2,1)S(1)}) custom-call(bf16[8,448]{1,0:T(8,128)(2,1)S(1)} %copy-done.3, bf16[8,448]{1,0:T(8,128)(2,1)S(1)} %copy-done.4, s32[8,8]{1,0:T(8,128)S(1)} %copy-done.6, ...), custom_call_target="tpu_custom_call" | custom-call | tf_op jit(solution)/shard_map/pallas_call | solution.py:424
  76.3 1.4 %shard_map.120 = (bf16[8,448]{1,0:T(8,128)(2,1)}, bf16[8,448]{1,0:T(8,128)(2,1)}, f32[112,1536]{1,0:T(8,128)}, f32[112,1536]{1,0:T(8,128)}, f32[112,1536]{1,0:T(8,128)}) custom-call(bf16[8,448]{1,0:T(8,128)(2,1)S(1)} %get-tuple-element.15.mixed_ref, bf16[8,448]{1,0:T(8,128)(2,1)S(1)} %get-tuple-element.16.dtok_ref, ...), custom_call_target="tpu_custom_call" | custom-call | tf_op jit(solution)/shard_map/pallas_call | solution.py:462
Async XLA Ops:
  0.6 0.7 copy-start.7
  1.3 1.0 %copy-start = (bf16[112,1536]{1,0:T(8,128)(2,1)S(1)}, bf16[112,1536]{1,0:T(8,128)(2,1)}, u32[]{:S(2)}) copy-start(bf16[112,1536]{1,0:T(8,128)(2,1)} %gate_ref.1) | copy-start | bytes 1032196
  2.3 1.0 %copy-start.1 = (bf16[112,1536]{1,0:T(8,128)(2,1)S(1)}, bf16[112,1536]{1,0:T(8,128)(2,1)}, u32[]{:S(2)}) copy-start(bf16[112,1536]{1,0:T(8,128)(2,1)} %up_ref.1) | copy-start | bytes 1032196
  3.2 1.0 %copy-start.2 = (bf16[1536,112]{0,1:T(8,128)(2,1)S(1)}, bf16[1536,112]{0,1:T(8,128)(2,1)}, u32[]{:S(2)}) copy-start(bf16[1536,112]{0,1:T(8,128)(2,1)} %param.12) | copy-start | bytes 1032196
  4.2 0.7 copy-start.3
  4.9 0.7 copy-start.4
  5.6 0.7 copy-start.5
  6.3 0.7 copy-start.6

commit v5 on v4

--- a/solution.py
+++ b/solution.py
@@ -9,6 +9,7 @@
 
 BLK = 128
 MESH = pl.DeviceIdType.MESH
+LIMIT = 60 * 1024 * 1024
 HALF, FULL = jnp.bfloat16, jnp.float32
 
 
@@ -23,10 +24,11 @@
 
 def kernel(
     nj, ny, nc, per,
-    tok_ref, cot_ref, routes_ref, map_ref, gates_ref, gate_ref, up_ref, down_ref,
+    tok_hbm, cot_hbm, routes_hbm, map_hbm, gates_hbm, gate_ref, up_ref, down_ref,
     mixed_ref, dtok_ref, gate_out, up_out, down_out,
     xs, xt, xb, dyb, xtr, dytr, wts, wbuf, wall, part, rs_buf, rs_recv, ag, grads, acc,
     op_send, op_core, op_buf, op_recv, t_send, t_recv,
+    tok_ref, cot_ref, routes_ref, map_ref, gates_ref, in_s, own_s,
     xt_ss, xt_rs, xb_ss, xb_rs, xc_ss, wt_ss, wt_rs, wl_s, w_ss, w_rs, r_ss, r_rs, a_ss, a_rs, g_ss, g_rs,
     oc_ss, oc_rs, o_ss, o_rs, t_ss, t_rs,
 ):
@@ -38,7 +40,7 @@
     z, y = e // ny, lax.rem(e, ny)
     rows = gate_ref.shape[0]
     quarter = gate_ref.shape[1] // ny
-    feats, padded = tok_ref.shape[1], xs.shape[1]
+    feats, padded = tok_hbm.shape[1], xs.shape[1]
     group = 8 * ny
     tokens_all = nj * group
 
@@ -84,6 +86,15 @@
         return pltpu.make_async_remote_copy(
             src_ref=src, dst_ref=dst, send_sem=ss, recv_sem=rs, device_id=device, device_id_type=MESH
         )
+
+    small = [
+        pltpu.make_async_copy(source, target, in_s.at[i])
+        for i, (source, target) in enumerate(
+            ((tok_hbm, tok_ref), (cot_hbm, cot_ref), (routes_hbm, routes_ref), (map_hbm, map_ref), (gates_hbm, gates_ref))
+        )
+    ]
+    for copy in small:
+        copy.start()
 
     barrier = pltpu.get_barrier_semaphore()
 
@@ -105,6 +116,8 @@
 
         lax.fori_loop(0, ny, step, 0)
 
+    for copy in small:
+        copy.wait()
     xs[...] = widen(jnp.concatenate([tok_ref[...].astype(FULL), cot_ref[...].astype(FULL)], axis=0), padded)
 
     @pl.when(z != j)
@@ -161,6 +174,27 @@
         for copy in copies:
             copy.wait_send()
 
+    experts = map_ref.shape[1]
+    names = lax.broadcasted_iota(jnp.int32, (8, experts), 1)
+    named = jnp.zeros((8, experts), FULL)
+    for k in range(routes_ref.shape[1]):
+        named = named + jnp.where(routes_ref[:, k : k + 1] == names, gates_ref[:, k : k + 1], 0.0)
+    picks = [map_ref[pl.ds(j * per + q, 1), :] - j * (ny * nc) for q in range(per)]
+    for k in range(ny):
+        for c in range(nc):
+            takes = sum((pick == k * nc + c).astype(FULL) for pick in picks)
+            weight = jnp.sum(named * takes, axis=1, keepdims=True)
+            wts[k, :, c * BLK : (c + 1) * BLK] = jnp.broadcast_to(weight, (8, BLK))
+
+    def wt_copy(k):
+        return remote(wts.at[k], wbuf.at[y], wt_ss.at[k], wt_rs.at[y], at_y(k))
+
+    def wt_wait(k):
+        return remote(wts.at[k], wbuf.at[k], wt_ss.at[k], wt_rs.at[k], at_y(k))
+
+    others(ny, y, lambda k: wt_copy(k).start())
+    wbuf[y] = wts[y]
+
     others(ny, y, lambda k: start_all(w_copies(k, 0, y)))
 
     crossing(lambda k: x_wait(k).wait_recv(), None)
@@ -183,32 +217,12 @@
     for c in range(nc):
         start_all(w_local(c))
 
-    experts = map_ref.shape[1]
-    names = lax.broadcasted_iota(jnp.int32, (8, experts), 1)
-    named = jnp.zeros((8, experts), FULL)
-    for k in range(routes_ref.shape[1]):
-        named = named + jnp.where(routes_ref[:, k : k + 1] == names, gates_ref[k], 0.0)
-    picks = [map_ref[pl.ds(j * per + q, 1), :] - j * (ny * nc) for q in range(per)]
-    for k in range(ny):
-        for c in range(nc):
-            takes = sum((pick == k * nc + c).astype(FULL) for pick in picks)
-            weight = jnp.sum(named * takes, axis=1, keepdims=True)
-            wts[k, :, c * BLK : (c + 1) * BLK] = jnp.broadcast_to(weight, (8, BLK))
-
-    def wt_copy(k):
-        return remote(wts.at[k], wbuf.at[y], wt_ss.at[k], wt_rs.at[y], at_y(k))
-
-    def wt_wait(k):
-        return remote(wts.at[k], wbuf.at[k], wt_ss.at[k], wt_rs.at[k], at_y(k))
-
-    others(ny, y, lambda k: wt_copy(k).start())
-    wbuf[y] = wts[y]
-
     def forward(k):
         xb_copy(k, 2 * k + core).wait_recv()
         xc_copy(k, core).start()
 
-    others(nx, x_me, forward)
+    for k in sorted(range(1, nx), key=lambda k: min(k, nx - k)):
+        forward(lax.rem(x_me + k, nx))
 
     def from_core(k, _):
         xc_copy(k, 1 - core).wait_recv()
@@ -245,6 +259,12 @@
         return [
             remote(grads.at[c, band(k), pl.ds(i * BLK, BLK)], ref.at[:, columns(slot, c)],
                    g_ss.at[c, i, k], g_rs.at[c, i, slot], at_y(k))
+            for i, ref in enumerate((gate_out, up_out, down_out))
+        ]
+
+    def g_local(c):
+        return [
+            pltpu.make_async_copy(grads.at[c, band(y), pl.ds(i * BLK, BLK)], ref.at[:, columns(y, c)], own_s.at[c, i])
             for i, ref in enumerate((gate_out, up_out, down_out))
         ]
 
@@ -283,6 +303,7 @@
             grads[c, :, 0 : 2 * BLK] = contract(xtr[...], pair, 1, 0).astype(HALF)
             grads[c, :, 2 * BLK : 3 * BLK] = contract(dytr[...], hidden, 1, 0).astype(HALF)
             others(ny, y, lambda k: start_all(g_copies(k, c, y)))
+            start_all(g_local(c))
 
         if c < nc - 1:
             block_grads()
@@ -296,7 +317,8 @@
         else:
             parts = jnp.concatenate([out_part, in_part], axis=1).reshape(nx, 2, group, 2 * feats)
             op_send[...] = parts.astype(HALF)
-            others(nx, x_me, lambda k: oc_copy(k).start())
+            for k in sorted(range(1, nx), key=lambda k: -min(k, nx - k)):
+                oc_copy(lax.rem(x_me + k, nx)).start()
             oc_copy(x_me).start()
             block_grads()
 
@@ -345,11 +367,9 @@
         op_buf[k] = (op_send[k, core].astype(FULL) + op_core[k].astype(FULL)).astype(HALF)
         op_copy(k, x_me).start()
 
-    others(nx, x_me, pass_on)
+    for k in sorted(range(1, nx), key=lambda k: -min(k, nx - k)):
+        pass_on(lax.rem(x_me + k, nx))
     oc_copy(x_me).wait_recv()
-    for c in range(nc):
-        for i, ref in enumerate((gate_out, up_out, down_out)):
-            ref[:, columns(y, c)] = grads[c, band(y), i * BLK : (i + 1) * BLK]
     op_recv[x_me] = op_core[x_me]
     others(nx, x_me, lambda k: op_copy(k, k).wait_recv())
     summed = jnp.sum(op_recv[...].astype(FULL), axis=0) + op_send[x_me, core].astype(FULL)
@@ -387,6 +407,7 @@
                 rs_copy(c, down, s).wait_send()
                 ag_copy(c, not down, s, False).wait_send()
         others(ny, y, lambda k: send_all(g_copies(k, c, y)))
+        wait_all(g_local(c))
 
     crossing(lambda k: t_wait(k).wait_recv(), None)
     final = jnp.sum(t_recv[...].astype(FULL), axis=0)
@@ -415,7 +436,6 @@
     hops = nj - 1
     dma = pltpu.SemaphoreType.DMA
     vmem = pl.BlockSpec(memory_space=pltpu.VMEM)
-    smem = pl.BlockSpec(memory_space=pltpu.SMEM)
     hbm = pl.BlockSpec(memory_space=pltpu.HBM)
     outs = (
         jax.ShapeDtypeStruct((tok, feats), HALF),
@@ -424,8 +444,8 @@
     results = pl.pallas_call(
         functools.partial(kernel, nj, ny, nc, per),
         out_shape=outs,
-        in_specs=[vmem] * 4 + [smem] + [hbm] * 3,
-        out_specs=(vmem,) * 5,
+        in_specs=[hbm] * 8,
+        out_specs=(vmem,) * 2 + (hbm,) * 3,
         scratch_shapes=[
             pltpu.VMEM((2 * tok, padded), HALF),
             pltpu.VMEM((ny, 2 * tok, padded), HALF),
@@ -448,6 +468,12 @@
             pltpu.VMEM((nx, group, 2 * feats), HALF),
             pltpu.VMEM((ny, 2 * tok, padded), HALF),
             pltpu.VMEM((ny, 2 * tok, padded), HALF),
+            pltpu.VMEM((tok, feats), HALF),
+            pltpu.VMEM((tok, feats), HALF),
+            pltpu.VMEM(routes.shape, jnp.int32),
+            pltpu.VMEM(block_map.shape[::-1], jnp.int32),
+            pltpu.VMEM((1, routes.shape[1]), FULL),
+            dma((5,)), dma((nc, 3)),
             dma((ny,)), dma((ny,)), dma((nx,)), dma((nj,)), dma((nx,)),
             dma((ny,)), dma((ny,)), dma((nc, 3)),
             dma((nc, 3, ny)), dma((nc, 3, ny)),
@@ -456,15 +482,19 @@
             dma((nx,)), dma((nx,)), dma((nx,)), dma((nx,)), dma((ny,)), dma((ny,)),
         ],
         compiler_params=pltpu.CompilerParams(
-            collective_id=0, has_side_effects=True, vmem_limit_bytes=40 * 1024 * 1024
+            collective_id=0, has_side_effects=True, vmem_limit_bytes=LIMIT
         ),
-    )(tokens, d_out, routes, block_map.T, route_gates, gate_dense, up_dense, down_dense.T)
+    )(tokens, d_out, routes, block_map.T, route_gates.reshape(1, -1), gate_dense, up_dense, down_dense.T)
+    steps = 3
+    small_spec = pl.BlockSpec((tok, feats), lambda i: (0, 0))
+    wide = pl.BlockSpec((rows, width // steps), lambda i: (0, i))
     mixed, d_tokens, gate_grad, up_grad, down_grad = pl.pallas_call(
         finish,
+        grid=(steps,),
         out_shape=outs[:2] + (jax.ShapeDtypeStruct((rows, width), FULL),) * 3,
-        in_specs=[vmem] * 5,
-        out_specs=(vmem,) * 5,
-        compiler_params=pltpu.CompilerParams(vmem_limit_bytes=16 * 1024 * 1024),
+        in_specs=[small_spec] * 2 + [wide] * 3,
+        out_specs=(small_spec,) * 2 + (wide,) * 3,
+        compiler_params=pltpu.CompilerParams(vmem_limit_bytes=LIMIT),
     )(*results)
     return mixed, d_tokens, gate_grad, up_grad, down_grad.T
 

time: 78.1 us -> 73.3 us (0.939)
  the two profiles are of different devices: /device:TPU:7 before, /device:TPU:2 now
where the time goes in v5:
time: 73.3 us; the launch traced here: 72 us
  Pallas kernels  71.4 us (97%)
    pallas_call x1, Pallas kernels, shards(): pl.pallas_call(functools.partial(kernel, nj, ny, nc, per), out_shape=outs...  68 us
    pallas_call x1, Pallas kernels, shards(): pl.pallas_call(finish, grid=(steps,), out_shape=outs[:2] + (jax.ShapeDtyp...  3.42 us

profile of v5, /device:TPU:2, one launch (start us, length us, event | category | flops | bytes accessed | tf_op | source)
XLA Modules:
  0.0 72.0 jit_solution(1736870455223205375)
XLA Ops:
  0.6 68.0 %shard_map.119 = (bf16[8,448]{1,0:T(8,128)(2,1)}, bf16[8,448]{1,0:T(8,128)(2,1)}, bf16[112,1536]{1,0:T(8,128)(2,1)}, bf16[112,1536]{1,0:T(8,128)(2,1)}, bf16[112,1536]{1,0:T(8,128)(2,1)}) custom-call(bf16[8,448]{1,0:T(8,128)(2,1)} %tok_hbm.1, bf16[8,448]{1,0:T(8,128)(2,1)} %cot_hbm.1, s32[8,8]{1,0:T(8,128)} %routes_hbm.1, s32[16,32]{1,0:T(8,128)} %bitcast.5, ...), custom_call_target="tpu_custom_call" | custom-call | tf_op jit(solution)/shard_map/pallas_call | solution.py:444
  68.6 3.4 %shard_map.120 = (bf16[8,448]{1,0:T(8,128)(2,1)}, bf16[8,448]{1,0:T(8,128)(2,1)}, f32[112,1536]{1,0:T(8,128)}, f32[112,1536]{1,0:T(8,128)}, f32[112,1536]{1,0:T(8,128)}) custom-call(bf16[8,448]{1,0:T(8,128)(2,1)} %get-tuple-element.15.mixed_ref, bf16[8,448]{1,0:T(8,128)(2,1)} %get-tuple-element.16.dtok_ref, bf16[112,1536]{1,0:T(8,128)(2,1)} %get-tuple-element.17.gate_ref, ...), custom_call_target="tpu_custom_call" | custom-call | tf_op jit(solution)/shard_map/pallas_call | solution.py:491

commit v6 on v5

--- a/solution.py
+++ b/solution.py
@@ -33,7 +33,6 @@
     oc_ss, oc_rs, o_ss, o_rs, t_ss, t_rs,
 ):
     nz, nx = nj, nj // 2
-    hops_down, hops_up = nz // 2, nz - 1 - nz // 2
     j = lax.axis_index("dp")
     e = lax.axis_index("expert")
     x_me, core = j // 2, lax.rem(j, 2)
@@ -101,13 +100,6 @@
     def greet(device):
         pl.semaphore_signal(barrier, inc=1, device_id=device, device_id_type=MESH)
 
-    others(ny, y, lambda k: greet(at_y(k)))
-    greet(at_z(1))
-    greet(at_z(-1))
-    others(nx, x_me, lambda k: greet(at_x(k)))
-    greet(other_core)
-    count = (ny - 1) + 2 + (nx - 1) + 1
-
     @pl.when(z != j)
     def _():
         def step(k, _):
@@ -115,6 +107,13 @@
             return 0
 
         lax.fori_loop(0, ny, step, 0)
+
+    others(ny, y, lambda k: greet(at_y(k)))
+    for k in (2, -2, 1, -1):
+        greet(at_z(k))
+    others(nx, x_me, lambda k: greet(at_x(k)))
+    greet(other_core)
+    count = (ny - 1) + 4 + (nx - 1) + 1
 
     for copy in small:
         copy.wait()
@@ -234,26 +233,28 @@
     def x_all():
         return xb[:, :, :feats].reshape(tokens_all, feats)
 
-    def lane(down, s):
-        return s - 1 if down else hops_down + s - 1
-
-    def rs_copy(c, down, s):
-        i = lane(down, s)
-        return remote(rs_buf.at[c, i], rs_recv.at[c, i], r_ss.at[c, i], r_rs.at[c, i], at_z(-1 if down else 1))
-
-    def rs_send(c, down, s):
-        t = lax.rem(z - (hops_down - s + 1) + nz, nz) if down else lax.rem(z + (hops_up - s + 1), nz)
-        value = part[c, t]
-        if s > 1:
-            value = value + rs_recv[c, lane(down, s - 1)].astype(FULL)
-        rs_buf[c, lane(down, s)] = value.astype(HALF)
-        rs_copy(c, down, s).start()
-
-    def ag_copy(c, down, s, arriving):
-        i = lane(not down, s)
-        shift = s if arriving else s - 1
-        slot = lax.rem(z + shift, nz) if down else lax.rem(z - shift + nz, nz)
-        return remote(ag.at[c, slot], ag.at[c, slot], a_ss.at[c, i], a_rs.at[c, i], at_z(-1 if down else 1))
+    def place(k):
+        return lax.rem(z + k + nz, nz)
+
+    RS_TO = (-2, 1, -1, -2, 2, -1, 1)
+
+    def rs_copy(c, i):
+        return remote(rs_buf.at[c, i], rs_recv.at[c, i], r_ss.at[c, i], r_rs.at[c, i], at_z(RS_TO[i]))
+
+    def rs_send(c, i, target, *arrived):
+        value = part[c, place(target)]
+        for k in arrived:
+            rs_copy(c, k).wait_recv()
+            value = value + rs_recv[c, k].astype(FULL)
+        rs_buf[c, i] = value.astype(HALF)
+        rs_copy(c, i).start()
+
+    AG_TO = (2, -2, 1, -1, 2, 1, -1)
+    AG_FROM = (0, 0, 0, 0, -2, -2, 2)
+
+    def ag_copy(c, i, arriving=False):
+        origin = place(AG_FROM[i] - AG_TO[i]) if arriving else place(AG_FROM[i])
+        return remote(ag.at[c, origin], ag.at[c, origin], a_ss.at[c, i], a_rs.at[c, i], at_z(AG_TO[i]))
 
     def g_copies(k, c, slot):
         return [
@@ -273,16 +274,19 @@
         others(ny, y, lambda k: recv_all(w_copies(k, c, k)))
         part[c, :, :, 0 : 2 * BLK] = contract(x_all(), wall[c, :, 0 : 2 * BLK], 1, 0).reshape(nz, group, 2 * BLK)
         part[c, :, :, 2 * BLK : 3 * BLK] = contract(dyb[...], wall[c, :, 2 * BLK : 3 * BLK], 1, 0).reshape(nz, group, BLK)
-        rs_send(c, True, 1)
-        if hops_up:
-            rs_send(c, False, 1)
+        rs_send(c, 0, -4)
+        rs_send(c, 1, 3)
+        rs_send(c, 2, -3)
+        rs_send(c, 5, -1)
+        rs_send(c, 6, 1)
 
     def middle(c):
         if c == 0:
             others(ny, y, lambda k: wt_wait(k).wait_recv())
-        total = part[c, z] + rs_recv[c, lane(True, hops_down)].astype(FULL)
-        if hops_up:
-            total = total + rs_recv[c, lane(False, hops_up)].astype(FULL)
+        total = part[c, z]
+        for i in (5, 6, 4, 3):
+            rs_copy(c, i).wait_recv()
+            total = total + rs_recv[c, i].astype(FULL)
         gate_pre, up_pre, hidden_grad = total[:, :BLK], total[:, BLK : 2 * BLK], total[:, 2 * BLK :]
         weight = wbuf[:, :, c * BLK : (c + 1) * BLK].reshape(group, BLK)
         sigma = jax.nn.sigmoid(gate_pre)
@@ -291,9 +295,8 @@
         ag[c, z, :, 0:BLK] = (scaled * up_pre * sigma * (1.0 + gate_pre * (1.0 - sigma))).astype(HALF)
         ag[c, z, :, BLK : 2 * BLK] = (scaled * silu).astype(HALF)
         ag[c, z, :, 2 * BLK : 3 * BLK] = (weight * silu * up_pre).astype(HALF)
-        ag_copy(c, False, 1, False).start()
-        if hops_up:
-            ag_copy(c, True, 1, False).start()
+        for i in range(4):
+            ag_copy(c, i).start()
 
     def last(c):
         pair = ag[c, :, :, 0 : 2 * BLK].reshape(tokens_all, 2 * BLK)
@@ -331,34 +334,27 @@
     def stage(c, s):
         if s == 0:
             first(c)
-        elif s <= hops_down:
-            rs_copy(c, True, s).wait_recv()
-            if s < hops_down:
-                rs_send(c, True, s + 1)
-            if s <= hops_up:
-                rs_copy(c, False, s).wait_recv()
-                if s < hops_up:
-                    rs_send(c, False, s + 1)
-            if s == hops_down:
-                middle(c)
+        elif s == 1:
+            rs_send(c, 4, 2, 1)
+            rs_send(c, 3, -2, 2, 0)
+        elif s == 2:
+            middle(c)
+        elif s == 3:
+            ag_copy(c, 0, True).wait_recv()
+            ag_copy(c, 4).start()
+            ag_copy(c, 5).start()
+            ag_copy(c, 1, True).wait_recv()
+            ag_copy(c, 6).start()
         else:
-            s = s - hops_down
-            ag_copy(c, False, s, True).wait_recv()
-            if s < hops_down:
-                ag_copy(c, False, s + 1, False).start()
-            if s <= hops_up:
-                ag_copy(c, True, s, True).wait_recv()
-                if s < hops_up:
-                    ag_copy(c, True, s + 1, False).start()
-            if s == hops_down:
-                last(c)
-
-    stages = 2 * hops_down + 1
-    for slot in range(stages + nc - 1):
-        for c in reversed(range(nc)):
-            if 0 <= slot - c < stages:
-                stage(c, slot - c)
-        if slot == nc - 1:
+            for i in (2, 3, 5, 6, 4):
+                ag_copy(c, i, True).wait_recv()
+            last(c)
+
+    stages = 5
+    for s in range(stages):
+        for c in range(nc):
+            stage(c, s)
+        if s == 0:
             xtr[...] = x_all().T
             dytr[...] = dyb[...].T
 
@@ -402,10 +398,9 @@
     others(nx, x_me, lambda k: op_copy(k, x_me).wait_send())
     for c in range(nc):
         others(ny, y, lambda k: send_all(w_copies(k, c, y)))
-        for down, hops in ((True, hops_down), (False, hops_up)):
-            for s in range(1, hops + 1):
-                rs_copy(c, down, s).wait_send()
-                ag_copy(c, not down, s, False).wait_send()
+        for i in range(nz - 1):
+            rs_copy(c, i).wait_send()
+            ag_copy(c, i).wait_send()
         others(ny, y, lambda k: send_all(g_copies(k, c, y)))
         wait_all(g_local(c))
 
@@ -416,11 +411,37 @@
     crossing(lambda k: t_copy(k).wait_send(), None)
 
 
-def finish(mixed_ref, dtok_ref, gate_ref, up_ref, down_ref, mixed_out, dtok_out, gate_out, up_out, down_out):
-    mixed_out[...] = mixed_ref[...]
-    dtok_out[...] = dtok_ref[...]
-    for source, target in ((gate_ref, gate_out), (up_ref, up_out), (down_ref, down_out)):
-        target[...] = source[...].astype(FULL)
+def finish(mixed_ref, dtok_ref, gate_ref, up_ref, down_ref, mixed_out, dtok_out, gate_out, up_out, down_out,
+           small, halves, fulls, in_s, out_s):
+    _, steps, _, width = halves.shape
+    moved = [
+        (pltpu.make_async_copy(source, small.at[i], in_s.at[i, 0]), pltpu.make_async_copy(small.at[i], target, out_s.at[i, 0]))
+        for i, (source, target) in enumerate(((mixed_ref, mixed_out), (dtok_ref, dtok_out)))
+    ]
+    wide = [(gate_ref, gate_out), (up_ref, up_out), (down_ref, down_out)]
+
+    def load(i, k):
+        return pltpu.make_async_copy(wide[i][0].at[:, pl.ds(k * width, width)], halves.at[i, k], in_s.at[2 + i, k])
+
+    def store(i, k):
+        return pltpu.make_async_copy(fulls.at[i, k], wide[i][1].at[:, pl.ds(k * width, width)], out_s.at[2 + i, k])
+
+    parts = [(i, k) for i in range(3) for k in range(steps)]
+    for i, k in parts:
+        load(i, k).start()
+    for source, _ in moved:
+        source.start()
+    for i, k in parts:
+        load(i, k).wait()
+        fulls[i, k] = halves[i, k].astype(FULL)
+        store(i, k).start()
+    for source, target in moved:
+        source.wait()
+        target.start()
+    for _, target in moved:
+        target.wait()
+    for i, k in parts:
+        store(i, k).wait()
 
 
 def shards(tokens, d_out, gate_dense, up_dense, down_dense, block_map, routes, route_gates):
@@ -485,15 +506,19 @@
             collective_id=0, has_side_effects=True, vmem_limit_bytes=LIMIT
         ),
     )(tokens, d_out, routes, block_map.T, route_gates.reshape(1, -1), gate_dense, up_dense, down_dense.T)
-    steps = 3
-    small_spec = pl.BlockSpec((tok, feats), lambda i: (0, 0))
-    wide = pl.BlockSpec((rows, width // steps), lambda i: (0, i))
+    steps = 2
     mixed, d_tokens, gate_grad, up_grad, down_grad = pl.pallas_call(
         finish,
-        grid=(steps,),
         out_shape=outs[:2] + (jax.ShapeDtypeStruct((rows, width), FULL),) * 3,
-        in_specs=[small_spec] * 2 + [wide] * 3,
-        out_specs=(small_spec,) * 2 + (wide,) * 3,
+        in_specs=[hbm] * 5,
+        out_specs=(hbm,) * 5,
+        scratch_shapes=[
+            pltpu.VMEM((2, tok, feats), HALF),
+            pltpu.VMEM((3, steps, rows, width // steps), HALF),
+            pltpu.VMEM((3, steps, rows, width // steps), FULL),
+            dma((5, steps)),
+            dma((5, steps)),
+        ],
         compiler_params=pltpu.CompilerParams(vmem_limit_bytes=LIMIT),
     )(*results)
     return mixed, d_tokens, gate_grad, up_grad, down_grad.T

time: 73.3 us -> 65.4 us (0.89)
  the two profiles are of different devices: /device:TPU:2 before, /device:TPU:15 now
where the time goes in v6:
time: 65.4 us; the launch traced here: 65.2 us
  Pallas kernels  64.6 us (99%)
    pallas_call x1, Pallas kernels, shards(): pl.pallas_call(functools.partial(kernel, nj, ny, nc, per), out_shape=outs...  62.1 us
    pallas_call x1, Pallas kernels, shards(): pl.pallas_call(finish, out_shape=outs[:2] + (jax.ShapeDtypeStruct((rows,...  2.42 us

profile of v6, /device:TPU:15, one launch (start us, length us, event | category | flops | bytes accessed | tf_op | source)
XLA Modules:
  0.0 65.2 jit_solution(2079022590905048201)
XLA Ops:
  0.6 62.1 %shard_map.119 = (bf16[8,448]{1,0:T(8,128)(2,1)}, bf16[8,448]{1,0:T(8,128)(2,1)}, bf16[112,1536]{1,0:T(8,128)(2,1)}, bf16[112,1536]{1,0:T(8,128)(2,1)}, bf16[112,1536]{1,0:T(8,128)(2,1)}) custom-call(bf16[8,448]{1,0:T(8,128)(2,1)} %tok_hbm.1, bf16[8,448]{1,0:T(8,128)(2,1)} %cot_hbm.1, s32[8,8]{1,0:T(8,128)} %routes_hbm.1, s32[16,32]{1,0:T(8,128)} %bitcast.5, ...), custom_call_target="tpu_custom_call" | custom-call | tf_op jit(solution)/shard_map/pallas_call | solution.py:465
  62.8 2.4 %shard_map.120 = (bf16[8,448]{1,0:T(8,128)(2,1)}, bf16[8,448]{1,0:T(8,128)(2,1)}, f32[112,1536]{1,0:T(8,128)}, f32[112,1536]{1,0:T(8,128)}, f32[112,1536]{1,0:T(8,128)}) custom-call(bf16[8,448]{1,0:T(8,128)(2,1)} %get-tuple-element.15.mixed_ref, bf16[8,448]{1,0:T(8,128)(2,1)} %get-tuple-element.16.dtok_ref, bf16[112,1536]{1,0:T(8,128)(2,1)} %get-tuple-element.17.gate_ref, ...), custom_call_target="tpu_custom_call" | custom-call | tf_op jit(solution)/shard_map/pallas_call | solution.py:510

commit v7 on v6

--- a/solution.py
+++ b/solution.py
@@ -10,6 +10,7 @@
 BLK = 128
 MESH = pl.DeviceIdType.MESH
 LIMIT = 60 * 1024 * 1024
+ORDER = "f0 f1 f2 t0 a0 a1 a2 m0 m1 m2 b0 b1 b2 r0 g0 o0 r1 g1 o1 r2 o2 g2"
 HALF, FULL = jnp.bfloat16, jnp.float32
 
 
@@ -52,8 +53,22 @@
     def at_x(k):
         return (2 * k + core, e)
 
-    def at_t(k):
-        return (z, j * ny + k)
+    def pick(values, index):
+        return sum(jnp.where(index == i, value, 0) for i, value in enumerate(values))
+
+    def slot_of(device):
+        ahead = lax.rem(device // 2 - z // 2 + nx, nx)
+        return lax.rem(z + pick((4, 3, 5, 2, 1, 0, 6, 7), 2 * ahead + lax.rem(device, 2)), nz)
+
+    mine = slot_of(j)
+    ahead = lax.rem(z - j + nz, nz)
+    keeper = 2 * lax.rem(j // 2 + pick((2, 2, 1, 0, 0, 1, 3, 3), ahead), nx) + pick((1, 0, 1, 1, 0, 0, 0, 1), ahead)
+
+    def at_keeper(k):
+        return (keeper, j * ny + k)
+
+    def at_source(k):
+        return (z, mine * ny + k)
 
     other_core = (2 * x_me + 1 - core, e)
 
@@ -64,19 +79,9 @@
 
         lax.fori_loop(1, n, step, 0)
 
-    def crossing(body, own):
+    def each_y(body):
         def step(k, _):
-            same = jnp.logical_and(z == j, k == y)
-
-            @pl.when(jnp.logical_not(same))
-            def _():
-                body(k)
-
-            if own is not None:
-                @pl.when(same)
-                def _():
-                    own(k)
-
+            body(k)
             return 0
 
         lax.fori_loop(0, ny, step, 0)
@@ -100,43 +105,28 @@
     def greet(device):
         pl.semaphore_signal(barrier, inc=1, device_id=device, device_id_type=MESH)
 
-    @pl.when(z != j)
-    def _():
-        def step(k, _):
-            greet(at_t(k))
-            return 0
-
-        lax.fori_loop(0, ny, step, 0)
-
+    each_y(lambda k: greet(at_keeper(k)))
+    each_y(lambda k: greet(at_source(k)))
     others(ny, y, lambda k: greet(at_y(k)))
     for k in (2, -2, 1, -1):
         greet(at_z(k))
     others(nx, x_me, lambda k: greet(at_x(k)))
     greet(other_core)
-    count = (ny - 1) + 4 + (nx - 1) + 1
+    count = 2 * ny + (ny - 1) + 4 + (nx - 1) + 1
 
     for copy in small:
         copy.wait()
     xs[...] = widen(jnp.concatenate([tok_ref[...].astype(FULL), cot_ref[...].astype(FULL)], axis=0), padded)
 
-    @pl.when(z != j)
-    def _():
-        pl.semaphore_wait(barrier, count + ny)
-
-    @pl.when(z == j)
-    def _():
-        pl.semaphore_wait(barrier, count)
+    pl.semaphore_wait(barrier, count)
 
     def x_copy(k):
-        return remote(xs, xt.at[y], xt_ss.at[k], xt_rs.at[y], at_t(k))
+        return remote(xs, xt.at[y], xt_ss.at[k], xt_rs.at[y], at_keeper(k))
 
     def x_wait(k):
-        return remote(xs, xt.at[k], xt_ss.at[k], xt_rs.at[k], at_t(k))
-
-    def x_own(k):
-        xt[k] = xs[...]
-
-    crossing(lambda k: x_copy(k).start(), x_own)
+        return remote(xs, xt.at[k], xt_ss.at[k], xt_rs.at[k], at_source(k))
+
+    each_y(lambda k: x_copy(k).start())
 
     def columns(k, c):
         return pl.ds(pl.multiple_of(k * quarter + c * BLK, BLK), BLK)
@@ -196,9 +186,9 @@
 
     others(ny, y, lambda k: start_all(w_copies(k, 0, y)))
 
-    crossing(lambda k: x_wait(k).wait_recv(), None)
+    each_y(lambda k: x_wait(k).wait_recv())
     landed = xt[...].astype(FULL)[:, :, :feats]
-    xb[j] = jnp.concatenate(
+    xb[mine] = jnp.concatenate(
         [landed[:, :8].reshape(group, feats), landed[:, 8:].reshape(group, feats)], axis=1
     ).astype(HALF)
 
@@ -206,10 +196,10 @@
         return remote(xb.at[slot], xb.at[slot], xb_ss.at[k], xb_rs.at[slot], at_x(k))
 
     def xc_copy(k, side):
-        slot = 2 * k + side
+        slot = slot_of(2 * k + side)
         return remote(xb.at[slot], xb.at[slot], xc_ss.at[k], xb_rs.at[slot], other_core)
 
-    others(nx, x_me, lambda k: xb_copy(k, j).start())
+    others(nx, x_me, lambda k: xb_copy(k, mine).start())
     xc_copy(x_me, core).start()
     for c in range(1, nc):
         others(ny, y, lambda k: start_all(w_copies(k, c, y)))
@@ -217,7 +207,7 @@
         start_all(w_local(c))
 
     def forward(k):
-        xb_copy(k, 2 * k + core).wait_recv()
+        xb_copy(k, slot_of(2 * k + core)).wait_recv()
         xc_copy(k, core).start()
 
     for k in sorted(range(1, nx), key=lambda k: min(k, nx - k)):
@@ -236,25 +226,37 @@
     def place(k):
         return lax.rem(z + k + nz, nz)
 
-    RS_TO = (-2, 1, -1, -2, 2, -1, 1)
+    cut = group // 2
+    low, high, both = pl.ds(0, cut), pl.ds(cut, cut), pl.ds(0, group)
+    RS_TO = (-2, 1, -1, -2, 2, -1, 1, 2)
+    RS_ROWS = (low, both, both, both, both, both, both, high)
 
     def rs_copy(c, i):
-        return remote(rs_buf.at[c, i], rs_recv.at[c, i], r_ss.at[c, i], r_rs.at[c, i], at_z(RS_TO[i]))
-
-    def rs_send(c, i, target, *arrived):
+        return remote(rs_buf.at[c, i, RS_ROWS[i], :], rs_recv.at[c, i, RS_ROWS[i], :],
+                      r_ss.at[c, i], r_rs.at[c, i], at_z(RS_TO[i]))
+
+    def rs_send(c, i, target, piece=None, half=None):
         value = part[c, place(target)]
-        for k in arrived:
-            rs_copy(c, k).wait_recv()
-            value = value + rs_recv[c, k].astype(FULL)
+        if piece is not None:
+            rs_copy(c, half).wait_recv()
+            rs_copy(c, piece).wait_recv()
+            value = value + rs_recv[c, piece].astype(FULL)
+            extra = rs_recv[c, half, RS_ROWS[half], :].astype(FULL)
+            if half == 0:
+                value = jnp.concatenate([value[:cut] + extra, value[cut:]], axis=0)
+            else:
+                value = jnp.concatenate([value[:cut], value[cut:] + extra], axis=0)
         rs_buf[c, i] = value.astype(HALF)
         rs_copy(c, i).start()
 
-    AG_TO = (2, -2, 1, -1, 2, 1, -1)
-    AG_FROM = (0, 0, 0, 0, -2, -2, 2)
+    AG_TO = (2, -2, 1, -1, 2, 1, -1, -2)
+    AG_FROM = (0, 0, 0, 0, -2, -2, 2, 2)
+    AG_ROWS = (both, both, both, both, low, both, both, high)
 
     def ag_copy(c, i, arriving=False):
         origin = place(AG_FROM[i] - AG_TO[i]) if arriving else place(AG_FROM[i])
-        return remote(ag.at[c, origin], ag.at[c, origin], a_ss.at[c, i], a_rs.at[c, i], at_z(AG_TO[i]))
+        piece = ag.at[c, origin, AG_ROWS[i], :]
+        return remote(piece, piece, a_ss.at[c, i], a_rs.at[c, i], at_z(AG_TO[i]))
 
     def g_copies(k, c, slot):
         return [
@@ -274,7 +276,8 @@
         others(ny, y, lambda k: recv_all(w_copies(k, c, k)))
         part[c, :, :, 0 : 2 * BLK] = contract(x_all(), wall[c, :, 0 : 2 * BLK], 1, 0).reshape(nz, group, 2 * BLK)
         part[c, :, :, 2 * BLK : 3 * BLK] = contract(dyb[...], wall[c, :, 2 * BLK : 3 * BLK], 1, 0).reshape(nz, group, BLK)
-        rs_send(c, 0, -4)
+        rs_send(c, 0, 4)
+        rs_send(c, 7, 4)
         rs_send(c, 1, 3)
         rs_send(c, 2, -3)
         rs_send(c, 5, -1)
@@ -298,18 +301,19 @@
         for i in range(4):
             ag_copy(c, i).start()
 
-    def last(c):
+    def halves(c):
         pair = ag[c, :, :, 0 : 2 * BLK].reshape(tokens_all, 2 * BLK)
-        hidden = ag[c, :, :, 2 * BLK : 3 * BLK].reshape(tokens_all, BLK)
-
-        def block_grads():
-            grads[c, :, 0 : 2 * BLK] = contract(xtr[...], pair, 1, 0).astype(HALF)
-            grads[c, :, 2 * BLK : 3 * BLK] = contract(dytr[...], hidden, 1, 0).astype(HALF)
-            others(ny, y, lambda k: start_all(g_copies(k, c, y)))
-            start_all(g_local(c))
-
-        if c < nc - 1:
-            block_grads()
+        return pair, ag[c, :, :, 2 * BLK : 3 * BLK].reshape(tokens_all, BLK)
+
+    def block_grads(c):
+        pair, hidden = halves(c)
+        grads[c, :, 0 : 2 * BLK] = contract(xtr[...], pair, 1, 0).astype(HALF)
+        grads[c, :, 2 * BLK : 3 * BLK] = contract(dytr[...], hidden, 1, 0).astype(HALF)
+        others(ny, y, lambda k: start_all(g_copies(k, c, y)))
+        start_all(g_local(c))
+
+    def outputs(c):
+        pair, hidden = halves(c)
         out_part = contract(hidden, wall[c, :, 2 * BLK : 3 * BLK], 1, 1)
         in_part = contract(pair, wall[c, :, 0 : 2 * BLK], 1, 1)
         if c > 0:
@@ -318,49 +322,45 @@
         if c < nc - 1:
             acc[0], acc[1] = out_part, in_part
         else:
-            parts = jnp.concatenate([out_part, in_part], axis=1).reshape(nx, 2, group, 2 * feats)
+            parts = jnp.concatenate([out_part, in_part], axis=1).reshape(nj, group, 2 * feats)
             op_send[...] = parts.astype(HALF)
             for k in sorted(range(1, nx), key=lambda k: -min(k, nx - k)):
                 oc_copy(lax.rem(x_me + k, nx)).start()
             oc_copy(x_me).start()
-            block_grads()
 
     def oc_copy(k):
-        return remote(op_send.at[k, 1 - core], op_core.at[k], oc_ss.at[k], oc_rs.at[k], other_core)
+        return remote(op_send.at[slot_of(2 * k + 1 - core)], op_core.at[k], oc_ss.at[k], oc_rs.at[k], other_core)
 
     def op_copy(k, slot):
         return remote(op_buf.at[k], op_recv.at[slot], o_ss.at[k], o_rs.at[slot], at_x(k))
 
-    def stage(c, s):
-        if s == 0:
-            first(c)
-        elif s == 1:
-            rs_send(c, 4, 2, 1)
-            rs_send(c, 3, -2, 2, 0)
-        elif s == 2:
-            middle(c)
-        elif s == 3:
-            ag_copy(c, 0, True).wait_recv()
-            ag_copy(c, 4).start()
-            ag_copy(c, 5).start()
-            ag_copy(c, 1, True).wait_recv()
-            ag_copy(c, 6).start()
-        else:
-            for i in (2, 3, 5, 6, 4):
-                ag_copy(c, i, True).wait_recv()
-            last(c)
-
-    stages = 5
-    for s in range(stages):
-        for c in range(nc):
-            stage(c, s)
-        if s == 0:
-            xtr[...] = x_all().T
-            dytr[...] = dyb[...].T
+    def second(c):
+        rs_send(c, 4, 2, 1, 7)
+        rs_send(c, 3, -2, 2, 0)
+
+    def onward(c):
+        ag_copy(c, 0, True).wait_recv()
+        ag_copy(c, 4).start()
+        ag_copy(c, 5).start()
+        ag_copy(c, 1, True).wait_recv()
+        ag_copy(c, 6).start()
+        ag_copy(c, 7).start()
+
+    def arrived(c):
+        for i in (2, 3, 5, 6, 4, 7):
+            ag_copy(c, i, True).wait_recv()
+
+    def turned(c):
+        xtr[...] = x_all().T
+        dytr[...] = dyb[...].T
+
+    steps = dict(f=first, a=second, m=middle, b=onward, r=arrived, g=block_grads, o=outputs, t=turned)
+    for step in ORDER.split():
+        steps[step[0]](int(step[1]))
 
     def pass_on(k):
         oc_copy(k).wait_recv()
-        op_buf[k] = (op_send[k, core].astype(FULL) + op_core[k].astype(FULL)).astype(HALF)
+        op_buf[k] = (op_send[slot_of(2 * k + core)].astype(FULL) + op_core[k].astype(FULL)).astype(HALF)
         op_copy(k, x_me).start()
 
     for k in sorted(range(1, nx), key=lambda k: -min(k, nx - k)):
@@ -368,7 +368,7 @@
     oc_copy(x_me).wait_recv()
     op_recv[x_me] = op_core[x_me]
     others(nx, x_me, lambda k: op_copy(k, k).wait_recv())
-    summed = jnp.sum(op_recv[...].astype(FULL), axis=0) + op_send[x_me, core].astype(FULL)
+    summed = jnp.sum(op_recv[...].astype(FULL), axis=0) + op_send[mine].astype(FULL)
     t_send[...] = widen(
         jnp.concatenate(
             [summed[:, :feats].reshape(ny, 8, feats), summed[:, feats:].reshape(ny, 8, feats)], axis=1
@@ -377,38 +377,35 @@
     )
 
     def t_copy(k):
-        return remote(t_send.at[k], t_recv.at[y], t_ss.at[k], t_rs.at[y], at_t(k))
+        return remote(t_send.at[k], t_recv.at[y], t_ss.at[k], t_rs.at[y], at_source(k))
 
     def t_wait(k):
-        return remote(t_send.at[k], t_recv.at[k], t_ss.at[k], t_rs.at[k], at_t(k))
-
-    def t_own(k):
-        t_recv[k] = t_send[k]
-
-    crossing(lambda k: t_copy(k).start(), t_own)
+        return remote(t_send.at[k], t_recv.at[k], t_ss.at[k], t_rs.at[k], at_keeper(k))
+
+    each_y(lambda k: t_copy(k).start())
 
     for c in range(nc):
         others(ny, y, lambda k: recv_all(g_copies(k, c, k)))
-    crossing(lambda k: x_copy(k).wait_send(), None)
+    each_y(lambda k: x_copy(k).wait_send())
     others(ny, y, lambda k: wt_copy(k).wait_send())
-    others(nx, x_me, lambda k: xb_copy(k, j).wait_send())
+    others(nx, x_me, lambda k: xb_copy(k, mine).wait_send())
     for k in range(nx):
         xc_copy(k, core).wait_send()
         oc_copy(k).wait_send()
     others(nx, x_me, lambda k: op_copy(k, x_me).wait_send())
     for c in range(nc):
         others(ny, y, lambda k: send_all(w_copies(k, c, y)))
-        for i in range(nz - 1):
+        for i in range(nz):
             rs_copy(c, i).wait_send()
             ag_copy(c, i).wait_send()
         others(ny, y, lambda k: send_all(g_copies(k, c, y)))
         wait_all(g_local(c))
 
-    crossing(lambda k: t_wait(k).wait_recv(), None)
+    each_y(lambda k: t_wait(k).wait_recv())
     final = jnp.sum(t_recv[...].astype(FULL), axis=0)
     mixed_ref[...] = final[:8, :feats].astype(HALF)
     dtok_ref[...] = final[8:, :feats].astype(HALF)
-    crossing(lambda k: t_copy(k).wait_send(), None)
+    each_y(lambda k: t_copy(k).wait_send())
 
 
 def finish(mixed_ref, dtok_ref, gate_ref, up_ref, down_ref, mixed_out, dtok_out, gate_out, up_out, down_out,
@@ -454,7 +451,6 @@
     nc = width // BLK // ny
     group = tok * ny
     padded = -(-feats // BLK) * BLK
-    hops = nj - 1
     dma = pltpu.SemaphoreType.DMA
     vmem = pl.BlockSpec(memory_space=pltpu.VMEM)
     hbm = pl.BlockSpec(memory_space=pltpu.HBM)
@@ -478,12 +474,12 @@
             pltpu.VMEM((ny, tok, nc * BLK), FULL),
             pltpu.VMEM((nc, ny * rows, 3 * BLK), HALF),
             pltpu.VMEM((nc, nj, group, 3 * BLK), FULL),
-            pltpu.VMEM((nc, hops, group, 3 * BLK), HALF),
-            pltpu.VMEM((nc, hops, group, 3 * BLK), HALF),
+            pltpu.VMEM((nc, nj, group, 3 * BLK), HALF),
+            pltpu.VMEM((nc, nj, group, 3 * BLK), HALF),
             pltpu.VMEM((nc, nj, group, 3 * BLK), HALF),
             pltpu.VMEM((nc, ny * rows, 3 * BLK), HALF),
             pltpu.VMEM((2, nj * group, feats), FULL),
-            pltpu.VMEM((nx, 2, group, 2 * feats), HALF),
+            pltpu.VMEM((nj, group, 2 * feats), HALF),
             pltpu.VMEM((nx, group, 2 * feats), HALF),
             pltpu.VMEM((nx, group, 2 * feats), HALF),
             pltpu.VMEM((nx, group, 2 * feats), HALF),
@@ -498,7 +494,7 @@
             dma((ny,)), dma((ny,)), dma((nx,)), dma((nj,)), dma((nx,)),
             dma((ny,)), dma((ny,)), dma((nc, 3)),
             dma((nc, 3, ny)), dma((nc, 3, ny)),
-            dma((nc, hops)), dma((nc, hops)), dma((nc, hops)), dma((nc, hops)),
+            dma((nc, nj)), dma((nc, nj)), dma((nc, nj)), dma((nc, nj)),
             dma((nc, 3, ny)), dma((nc, 3, ny)),
             dma((nx,)), dma((nx,)), dma((nx,)), dma((nx,)), dma((ny,)), dma((ny,)),
         ],

time: 65.4 us -> 64.7 us (0.989)
  the two profiles are of different devices: /device:TPU:15 before, /device:TPU:2 now
where the time goes in v7:
time: 64.7 us; the launch traced here: 64 us
  Pallas kernels  63.4 us (98%)
    pallas_call x1, Pallas kernels, shards(): pl.pallas_call(functools.partial(kernel, nj, ny, nc, per), out_shape=outs...  61 us
    pallas_call x1, Pallas kernels, shards(): pl.pallas_call(finish, out_shape=outs[:2] + (jax.ShapeDtypeStruct((rows,...  2.42 us

profile of v7, /device:TPU:2, one launch (start us, length us, event | category | flops | bytes accessed | tf_op | source)
XLA Modules:
  0.0 64.0 jit_solution(1753952009521826850)
XLA Ops:
  0.6 61.0 %shard_map.119 = (bf16[8,448]{1,0:T(8,128)(2,1)}, bf16[8,448]{1,0:T(8,128)(2,1)}, bf16[112,1536]{1,0:T(8,128)(2,1)}, bf16[112,1536]{1,0:T(8,128)(2,1)}, bf16[112,1536]{1,0:T(8,128)(2,1)}) custom-call(bf16[8,448]{1,0:T(8,128)(2,1)} %tok_hbm.1, bf16[8,448]{1,0:T(8,128)(2,1)} %cot_hbm.1, s32[8,8]{1,0:T(8,128)} %routes_hbm.1, s32[16,32]{1,0:T(8,128)} %bitcast.5, ...), custom_call_target="tpu_custom_call" | custom-call | tf_op jit(solution)/shard_map/pallas_call | solution.py:461
  61.6 2.4 %shard_map.120 = (bf16[8,448]{1,0:T(8,128)(2,1)}, bf16[8,448]{1,0:T(8,128)(2,1)}, f32[112,1536]{1,0:T(8,128)}, f32[112,1536]{1,0:T(8,128)}, f32[112,1536]{1,0:T(8,128)}) custom-call(bf16[8,448]{1,0:T(8,128)(2,1)} %get-tuple-element.15.mixed_ref, bf16[8,448]{1,0:T(8,128)(2,1)} %get-tuple-element.16.dtok_ref, bf16[112,1536]{1,0:T(8,128)(2,1)} %get-tuple-element.17.gate_ref, ...), custom_call_target="tpu_custom_call" | custom-call | tf_op jit(solution)/shard_map/pallas_call | solution.py:506

commit v8 on v7

--- a/solution.py
+++ b/solution.py
@@ -10,7 +10,6 @@
 BLK = 128
 MESH = pl.DeviceIdType.MESH
 LIMIT = 60 * 1024 * 1024
-ORDER = "f0 f1 f2 t0 a0 a1 a2 m0 m1 m2 b0 b1 b2 r0 g0 o0 r1 g1 o1 r2 o2 g2"
 HALF, FULL = jnp.bfloat16, jnp.float32
 
 
@@ -73,11 +72,8 @@
     other_core = (2 * x_me + 1 - core, e)
 
     def others(n, me, body):
-        def step(i, _):
+        for i in sorted(range(1, n), key=lambda i: -min(i, n - i)):
             body(lax.rem(me + i, n))
-            return 0
-
-        lax.fori_loop(1, n, step, 0)
 
     def each_y(body):
         def step(k, _):
@@ -350,13 +346,28 @@
         for i in (2, 3, 5, 6, 4, 7):
             ag_copy(c, i, True).wait_recv()
 
-    def turned(c):
+    def turned():
         xtr[...] = x_all().T
         dytr[...] = dyb[...].T
 
-    steps = dict(f=first, a=second, m=middle, b=onward, r=arrived, g=block_grads, o=outputs, t=turned)
-    for step in ORDER.split():
-        steps[step[0]](int(step[1]))
+    first(0)
+    first(1)
+    second(0)
+    for c in range(2, nc):
+        first(c)
+    for c in range(1, nc):
+        second(c)
+    for c in range(nc):
+        middle(c)
+    turned()
+    for c in range(nc):
+        onward(c)
+    for c in range(nc):
+        arrived(c)
+        if c < nc - 1:
+            block_grads(c)
+        outputs(c)
+    block_grads(nc - 1)
 
     def pass_on(k):
         oc_copy(k).wait_recv()

time: 64.7 us -> 63.2 us (0.977)
  Pallas kernels: 63.4 us -> 62.2 us
    pallas_call x1, Pallas kernels: 61 us -> 59.8 us  [shards(): pl.pallas_call(functools.partial(kernel, nj, ny, nc, per), out_shape=outs...]
where the time goes in v8:
time: 63.2 us; the launch traced here: 62.8 us
  Pallas kernels  62.2 us (98%)
  between operations  0.64 us (1%)
    pallas_call x1, Pallas kernels, shards(): pl.pallas_call(functools.partial(kernel, nj, ny, nc, per), out_shape=outs...  59.8 us
    pallas_call x1, Pallas kernels, shards(): pl.pallas_call(finish, out_shape=outs[:2] + (jax.ShapeDtypeStruct((rows,...  2.42 us

profile of v8, /device:TPU:2, one launch (start us, length us, event | category | flops | bytes accessed | tf_op | source)
XLA Modules:
  0.0 62.8 jit_solution(1264593377624982227)
XLA Ops:
  0.6 59.8 %shard_map.119 = (bf16[8,448]{1,0:T(8,128)(2,1)}, bf16[8,448]{1,0:T(8,128)(2,1)}, bf16[112,1536]{1,0:T(8,128)(2,1)}, bf16[112,1536]{1,0:T(8,128)(2,1)}, bf16[112,1536]{1,0:T(8,128)(2,1)}) custom-call(bf16[8,448]{1,0:T(8,128)(2,1)} %tok_hbm.1, bf16[8,448]{1,0:T(8,128)(2,1)} %cot_hbm.1, s32[8,8]{1,0:T(8,128)} %routes_hbm.1, s32[16,32]{1,0:T(8,128)} %bitcast.5, ...), custom_call_target="tpu_custom_call" | custom-call | tf_op jit(solution)/shard_map/pallas_call | solution.py:472
  60.4 2.4 %shard_map.120 = (bf16[8,448]{1,0:T(8,128)(2,1)}, bf16[8,448]{1,0:T(8,128)(2,1)}, f32[112,1536]{1,0:T(8,128)}, f32[112,1536]{1,0:T(8,128)}, f32[112,1536]{1,0:T(8,128)}) custom-call(bf16[8,448]{1,0:T(8,128)(2,1)} %get-tuple-element.15.mixed_ref, bf16[8,448]{1,0:T(8,128)(2,1)} %get-tuple-element.16.dtok_ref, bf16[112,1536]{1,0:T(8,128)(2,1)} %get-tuple-element.17.gate_ref, ...), custom_call_target="tpu_custom_call" | custom-call | tf_op jit(solution)/shard_map/pallas_call | solution.py:517

commit v9 on v8

--- a/solution.py
+++ b/solution.py
@@ -25,9 +25,9 @@
 def kernel(
     nj, ny, nc, per,
     tok_hbm, cot_hbm, routes_hbm, map_hbm, gates_hbm, gate_ref, up_ref, down_ref,
-    mixed_ref, dtok_ref, gate_out, up_out, down_out,
+    t_recv, gate_out, up_out, down_out,
     xs, xt, xb, dyb, xtr, dytr, wts, wbuf, wall, part, rs_buf, rs_recv, ag, grads, acc,
-    op_send, op_core, op_buf, op_recv, t_send, t_recv,
+    op_send, op_core, op_buf, op_recv, t_send,
     tok_ref, cot_ref, routes_ref, map_ref, gates_ref, in_s, own_s,
     xt_ss, xt_rs, xb_ss, xb_rs, xc_ss, wt_ss, wt_rs, wl_s, w_ss, w_rs, r_ss, r_rs, a_ss, a_rs, g_ss, g_rs,
     oc_ss, oc_rs, o_ss, o_rs, t_ss, t_rs,
@@ -413,18 +413,16 @@
         wait_all(g_local(c))
 
     each_y(lambda k: t_wait(k).wait_recv())
-    final = jnp.sum(t_recv[...].astype(FULL), axis=0)
-    mixed_ref[...] = final[:8, :feats].astype(HALF)
-    dtok_ref[...] = final[8:, :feats].astype(HALF)
     each_y(lambda k: t_copy(k).wait_send())
 
 
-def finish(mixed_ref, dtok_ref, gate_ref, up_ref, down_ref, mixed_out, dtok_out, gate_out, up_out, down_out,
-           small, halves, fulls, in_s, out_s):
+def finish(parts_ref, gate_ref, up_ref, down_ref, mixed_out, dtok_out, gate_out, up_out, down_out,
+           pieces, small, halves, fulls, in_s, out_s):
     _, steps, _, width = halves.shape
-    moved = [
-        (pltpu.make_async_copy(source, small.at[i], in_s.at[i, 0]), pltpu.make_async_copy(small.at[i], target, out_s.at[i, 0]))
-        for i, (source, target) in enumerate(((mixed_ref, mixed_out), (dtok_ref, dtok_out)))
+    _, tok, feats = small.shape
+    arrive = pltpu.make_async_copy(parts_ref, pieces, in_s.at[0, 0])
+    leave = [
+        pltpu.make_async_copy(small.at[i], target, out_s.at[i, 0]) for i, target in enumerate((mixed_out, dtok_out))
     ]
     wide = [(gate_ref, gate_out), (up_ref, up_out), (down_ref, down_out)]
 
@@ -434,20 +432,21 @@
     def store(i, k):
         return pltpu.make_async_copy(fulls.at[i, k], wide[i][1].at[:, pl.ds(k * width, width)], out_s.at[2 + i, k])
 
+    arrive.start()
     parts = [(i, k) for i in range(3) for k in range(steps)]
     for i, k in parts:
         load(i, k).start()
-    for source, _ in moved:
-        source.start()
+    arrive.wait()
+    final = jnp.sum(pieces[...].astype(FULL), axis=0)
+    for i in range(2):
+        small[i] = final[i * tok : (i + 1) * tok, :feats].astype(HALF)
+        leave[i].start()
     for i, k in parts:
         load(i, k).wait()
         fulls[i, k] = halves[i, k].astype(FULL)
         store(i, k).start()
-    for source, target in moved:
-        source.wait()
-        target.start()
-    for _, target in moved:
-        target.wait()
+    for copy in leave:
+        copy.wait()
     for i, k in parts:
         store(i, k).wait()
 
@@ -463,17 +462,13 @@
     group = tok * ny
     padded = -(-feats // BLK) * BLK
     dma = pltpu.SemaphoreType.DMA
-    vmem = pl.BlockSpec(memory_space=pltpu.VMEM)
     hbm = pl.BlockSpec(memory_space=pltpu.HBM)
-    outs = (
-        jax.ShapeDtypeStruct((tok, feats), HALF),
-        jax.ShapeDtypeStruct((tok, feats), HALF),
-    ) + (jax.ShapeDtypeStruct((rows, width), HALF),) * 3
+    outs = (jax.ShapeDtypeStruct((ny, 2 * tok, padded), HALF),) + (jax.ShapeDtypeStruct((rows, width), HALF),) * 3
     results = pl.pallas_call(
         functools.partial(kernel, nj, ny, nc, per),
         out_shape=outs,
         in_specs=[hbm] * 8,
-        out_specs=(vmem,) * 2 + (hbm,) * 3,
+        out_specs=(hbm,) * 4,
         scratch_shapes=[
             pltpu.VMEM((2 * tok, padded), HALF),
             pltpu.VMEM((ny, 2 * tok, padded), HALF),
@@ -495,7 +490,6 @@
             pltpu.VMEM((nx, group, 2 * feats), HALF),
             pltpu.VMEM((nx, group, 2 * feats), HALF),
             pltpu.VMEM((ny, 2 * tok, padded), HALF),
-            pltpu.VMEM((ny, 2 * tok, padded), HALF),
             pltpu.VMEM((tok, feats), HALF),
             pltpu.VMEM((tok, feats), HALF),
             pltpu.VMEM(routes.shape, jnp.int32),
@@ -516,10 +510,11 @@
     steps = 2
     mixed, d_tokens, gate_grad, up_grad, down_grad = pl.pallas_call(
         finish,
-        out_shape=outs[:2] + (jax.ShapeDtypeStruct((rows, width), FULL),) * 3,
-        in_specs=[hbm] * 5,
+        out_shape=(jax.ShapeDtypeStruct((tok, feats), HALF),) * 2 + (jax.ShapeDtypeStruct((rows, width), FULL),) * 3,
+        in_specs=[hbm] * 4,
         out_specs=(hbm,) * 5,
         scratch_shapes=[
+            pltpu.VMEM((ny, 2 * tok, padded), HALF),
             pltpu.VMEM((2, tok, feats), HALF),
             pltpu.VMEM((3, steps, rows, width // steps), HALF),
             pltpu.VMEM((3, steps, rows, width // steps), FULL),

time: 63.2 us -> 63.2 us (level)
  no operation moved by 1% of the time
where the time goes in v9:
time: 63.2 us; the launch traced here: 62.5 us
  Pallas kernels  61.8 us (98%)
  between operations  0.64 us (1%)
    pallas_call x1, Pallas kernels, shards(): pl.pallas_call(functools.partial(kernel, nj, ny, nc, per), out_shape=outs...  59.4 us
    pallas_call x1, Pallas kernels, shards(): pl.pallas_call(finish, out_shape=(jax.ShapeDtypeStruct((tok, feats), HALF...  2.46 us

profile of v9, /device:TPU:2, one launch (start us, length us, event | category | flops | bytes accessed | tf_op | source)
XLA Modules:
  0.0 62.5 jit_solution(15959658052601568283)
XLA Ops:
  0.6 59.4 %shard_map.119 = (bf16[4,16,512]{2,1,0:T(8,128)(2,1)}, bf16[112,1536]{1,0:T(8,128)(2,1)}, bf16[112,1536]{1,0:T(8,128)(2,1)}, bf16[112,1536]{1,0:T(8,128)(2,1)}) custom-call(bf16[8,448]{1,0:T(8,128)(2,1)} %tok_hbm.1, bf16[8,448]{1,0:T(8,128)(2,1)} %cot_hbm.1, s32[8,8]{1,0:T(8,128)} %routes_hbm.1, s32[16,32]{1,0:T(8,128)} %bitcast.5, f32[1,8]{1,0:T(1,128)} %bitcast.6, ...), custom_call_target="tpu_custom_call" | custom-call | tf_op jit(solution)/shard_map/pallas_call | solution.py:467
  60.0 2.5 %shard_map.120 = (bf16[8,448]{1,0:T(8,128)(2,1)}, bf16[8,448]{1,0:T(8,128)(2,1)}, f32[112,1536]{1,0:T(8,128)}, f32[112,1536]{1,0:T(8,128)}, f32[112,1536]{1,0:T(8,128)}) custom-call(bf16[4,16,512]{2,1,0:T(8,128)(2,1)} %get-tuple-element.14.parts_ref, bf16[112,1536]{1,0:T(8,128)(2,1)} %get-tuple-element.15.gate_ref, ...), custom_call_target="tpu_custom_call" | custom-call | tf_op jit(solution)/shard_map/pallas_call | solution.py:511
